TPU v7x, 256 devices: a whole 4x4x8 slice. The times are simulated.
256 devices in a mesh: ctx: 32 (over z, x_hi, core), dp: 8 (over y, x_lo).
Axes of the slice: x: 4 (x_hi: 2, x_lo: 2; x = x_hi * 2 + x_lo), y: 4, z: 8, core: 2. Of those that a mesh axis runs over, the one named last changes fastest.
Arguments:
- query_act: bfloat16 [8, 16384, 512], P('dp', 'ctx'), may hold values from -6 to 6
- key_act: bfloat16 [8, 16384, 512], P('dp', 'ctx'), may hold values from -6 to 6
- value_act: bfloat16 [8, 16384, 512], P('dp', 'ctx'), may hold values from -6 to 6
- filter_taps: bfloat16 [128, 512], replicated, may hold values from -0.5 to 0.5
- grad_out: bfloat16 [8, 16384, 512], P('dp', 'ctx'), may hold values from -6 to 6
Outputs:
- grad_query: bfloat16 [8, 16384, 512], P('dp', 'ctx')
- grad_key: bfloat16 [8, 16384, 512], P('dp', 'ctx')
- grad_value: bfloat16 [8, 16384, 512], P('dp', 'ctx')
- grad_filter: float32 [128, 512], replicated
All inputs are finite; a program needn't handle non-finite values.
Results may differ from a plain program's by a relative error of at most 0.0052.
Values may be sent and summed in bfloat16 or wider, within the bound.
No kernel may reach another device: no remote copies, remote signals or barrier semaphores. Data moves between devices by JAX's collectives and lax.ppermute only.
A program may use at most 128 MiB of HBM per device.

v0:
```python
import math

import jax
import jax.numpy as jnp
from jax import lax
from jax.sharding import PartitionSpec as P


def passed_along(block, axis, distance):
    devices = range(lax.axis_size(axis))
    route = [(i - distance, i) for i in devices if i - distance in devices]
    return lax.ppermute(block, axis, route)


def block_matrices(taps_part, tap_count, block_size):
    piece_count = tap_count // block_size + 1
    steps_k = jnp.arange(piece_count)[:, None, None]
    rows_a = jnp.arange(block_size)[None, :, None]
    cols_b = jnp.arange(block_size)[None, None, :]
    offsets = steps_k * block_size + rows_a - cols_b
    valid = (offsets >= 0) & (offsets < tap_count)
    picked = taps_part[jnp.clip(offsets, 0, tap_count - 1)]
    zeroed = jnp.zeros_like(picked)
    return jnp.where(valid[:, :, :, None], picked, zeroed).transpose(0, 3, 1, 2)


def shards(query_act, key_act, value_act, filter_taps, grad_out):
    seq_count, row_count, chan_count = query_act.shape
    tap_count = filter_taps.shape[0]
    group_width = min(128, chan_count)
    conv_block = min(64, tap_count)
    piece_count = tap_count // conv_block
    conv_blocks = row_count // conv_block
    corr_block = min(32, tap_count)
    corr_pieces = tap_count // corr_block
    corr_blocks = row_count // corr_block
    gated = (key_act.astype(jnp.float32) * value_act.astype(jnp.float32)).astype(jnp.bfloat16)
    mix_grad = (grad_out.astype(jnp.float32) * query_act.astype(jnp.float32)).astype(jnp.bfloat16)
    edge_before = passed_along(gated[:, row_count - tap_count + 1 :, :], "ctx", 1)
    edge_after = passed_along(mix_grad[:, : tap_count - 1, :], "ctx", -1)
    zero_row = jnp.zeros((seq_count, 1, chan_count), jnp.bfloat16)
    padded_before = jnp.concatenate([zero_row, edge_before, gated], axis=1)
    padded_after = jnp.concatenate([mix_grad, edge_after, zero_row], axis=1)
    before_blocks = padded_before.reshape(
        seq_count, (row_count + tap_count) // conv_block, conv_block, chan_count
    )
    after_blocks = padded_after.reshape(
        seq_count, (row_count + tap_count) // conv_block, conv_block, chan_count
    )
    stack_before = jnp.stack(
        [
            before_blocks[:, piece_count - k : piece_count - k + conv_blocks]
            for k in range(piece_count + 1)
        ]
    )
    stack_before = stack_before.reshape(
        piece_count + 1, seq_count * conv_blocks, conv_block, chan_count
    )
    stack_after = jnp.stack([after_blocks[:, k : k + conv_blocks] for k in range(piece_count + 1)])
    stack_after = stack_after.reshape(
        piece_count + 1, seq_count * conv_blocks, conv_block, chan_count
    )
    corr_source = padded_before.reshape(
        seq_count, (row_count + tap_count) // corr_block, corr_block, chan_count
    )
    windows = jnp.concatenate(
        [corr_source[:, k : k + corr_blocks] for k in range(corr_pieces + 1)], axis=2
    )
    windows = windows.reshape(seq_count * corr_blocks, tap_count + corr_block, chan_count)
    grad_rows = mix_grad.reshape(seq_count * corr_blocks, corr_block, chan_count)
    row_ids = jnp.arange(corr_block)[:, None, None]
    col_ids = jnp.arange(tap_count + corr_block)[None, :, None]
    tap_ids = jnp.arange(tap_count)[None, None, :]
    selector = (col_ids == row_ids + tap_count - tap_ids).astype(jnp.float32)
    count_all = seq_count * row_count * lax.axis_size("ctx") * lax.axis_size("dp")

    def filter_part(first_chan):
        last_chan = first_chan + group_width
        product = jnp.einsum(
            "nac,nwc->caw",
            grad_rows[:, :, first_chan:last_chan],
            windows[:, :, first_chan:last_chan],
            preferred_element_type=jnp.float32,
        )
        return jnp.einsum("caw,awj->jc", product, selector, precision=lax.Precision.HIGHEST)

    def grad_part(first_chan):
        last_chan = first_chan + group_width
        mats = block_matrices(filter_taps[:, first_chan:last_chan], tap_count, conv_block)
        mixed = jnp.einsum(
            "knbc,kcab->nac",
            stack_before[:, :, :, first_chan:last_chan],
            mats,
            preferred_element_type=jnp.float32,
        )
        carried = jnp.einsum(
            "knbc,kcba->nac",
            stack_after[:, :, :, first_chan:last_chan],
            mats,
            preferred_element_type=jnp.float32,
        )
        shape_out = (seq_count, row_count, group_width)
        mixed = mixed.reshape(shape_out)
        carried = carried.reshape(shape_out)
        grad_q = (grad_out[:, :, first_chan:last_chan].astype(jnp.float32) * mixed).astype(
            jnp.bfloat16
        )
        grad_k = (carried * value_act[:, :, first_chan:last_chan].astype(jnp.float32)).astype(
            jnp.bfloat16
        )
        grad_v = (carried * key_act[:, :, first_chan:last_chan].astype(jnp.float32)).astype(
            jnp.bfloat16
        )
        return (grad_q, grad_k, grad_v)

    starts = list(range(0, chan_count, group_width))
    pieces = [grad_part(first) for first in starts]
    summed = lax.psum(
        jnp.concatenate([filter_part(first) for first in starts], axis=1), ("ctx", "dp")
    )
    grad_filter = summed / math.sqrt(count_all)
    grad_query = jnp.concatenate([piece[0] for piece in pieces], axis=2)
    grad_key = jnp.concatenate([piece[1] for piece in pieces], axis=2)
    grad_value = jnp.concatenate([piece[2] for piece in pieces], axis=2)
    return (grad_query, grad_key, grad_value, grad_filter)


def solution(mesh):
    return jax.shard_map(
        shards,
        mesh=mesh,
        in_specs=(
            P("dp", "ctx", None),
            P("dp", "ctx", None),
            P("dp", "ctx", None),
            P(),
            P("dp", "ctx", None),
        ),
        out_specs=(P("dp", "ctx", None), P("dp", "ctx", None), P("dp", "ctx", None), P()),
        check_vma=False,
    )
```

profile of v0, /device:TPU:1, one launch (start us, length us, event | category | flops | bytes accessed | tf_op | source)
XLA Modules:
  0.0 566.2 jit_solution(7509170428550440880)
XLA Ops:
  9.3 5.1 collective-permute-start.1
  17.3 2.8 collective-permute-start
  25.4 35.9 %gather_fusion = bf16[12288,128]{1,0:T(8,128)(2,1)S(1)} fusion(bf16[128,128]{1,0:T(8,128)(2,1)S(1)} %get-tuple-element.42, s32[12288]{0:T(1024)S(1)} %broadcast_clamp_fusion), kind=kCustom, calls=%fused_computation | custom fusion | bytes 6340608 | tf_op jit(solution)/shard_map/gather | solution.py:22
  61.4 9.2 %copy.32 = bf16[3,64,64,128]{2,1,0,3:T(8,128)(2,1)} copy(bf16[3,64,64,128]{3,2,1,0:T(8,128)(2,1)S(1)} %bitcast.169) | data formatting | bytes 6291456 | tf_op jit(solution)/shard_map/gather | solution.py:22
  70.6 35.9 %gather_fusion.1 = bf16[12288,128]{1,0:T(8,128)(2,1)S(1)} fusion(bf16[128,128]{1,0:T(8,128)(2,1)S(1)} %get-tuple-element.43, s32[12288]{0:T(1024)S(1)} %broadcast_clamp_fusion), kind=kCustom, calls=%fused_computation.1 | custom fusion | bytes 6340608 | tf_op jit(solution)/shard_map/gather | solution.py:22
  106.5 9.2 %copy.37 = bf16[3,64,64,128]{2,1,0,3:T(8,128)(2,1)} copy(bf16[3,64,64,128]{3,2,1,0:T(8,128)(2,1)S(1)} %bitcast.170) | data formatting | bytes 6291456 | tf_op jit(solution)/shard_map/gather | solution.py:22
  115.7 35.9 %gather_fusion.3 = bf16[12288,128]{1,0:T(8,128)(2,1)S(1)} fusion(bf16[128,128]{1,0:T(8,128)(2,1)S(1)} %get-tuple-element.44, s32[12288]{0:T(1024)S(1)} %broadcast_clamp_fusion), kind=kCustom, calls=%fused_computation.3 | custom fusion | bytes 6340608 | tf_op jit(solution)/shard_map/gather | solution.py:22
  151.7 43.3 %gather_fusion.2 = bf16[12288,128]{1,0:T(8,128)(2,1)} fusion(bf16[128,128]{1,0:T(8,128)(2,1)S(1)} %get-tuple-element.45, s32[12288]{0:T(1024)S(1)} %broadcast_clamp_fusion), kind=kCustom, calls=%fused_computation.2 | custom fusion | bytes 6340608 | tf_op jit(solution)/shard_map/gather | solution.py:22
  195.0 10.2 %copy.39 = bf16[3,64,64,128]{2,1,0,3:T(8,128)(2,1)} copy(bf16[3,64,64,128]{3,2,1,0:T(8,128)(2,1)} %bitcast.168) | data formatting | bytes 6291456 | tf_op jit(solution)/shard_map/gather | solution.py:22
  205.2 9.5 %copy.41 = bf16[3,64,64,128]{2,1,0,3:T(8,128)(2,1)} copy(bf16[3,64,64,128]{3,2,1,0:T(8,128)(2,1)S(1)} %bitcast.167) | data formatting | bytes 6291456 | tf_op jit(solution)/shard_map/gather | solution.py:22
  222.6 2.7 copy.71
  225.3 2.7 copy.72
  232.8 5.8 %fusion.39 = f32[8,64,128]{1,0,2:T(8,128)} fusion(bf16[3,64,64,128]{2,1,0,3:T(8,128)(2,1)} %copy.32, pred[3,64,64]{2,1,0:T(8,128)(4,1)S(1)} %fusion.94, bf16[3,8,64,512]{2,1,0,3:T(8,128)(2,1)S(1)} %maximum_bitcast_fusion.1), kind=kOutput, calls=%fused_computation.48 | convolution fusion | flops 26738688 | bytes 4218880 | tf_op jit(solution)/shard_map/knbc,kcba->nac/dot_general | solution.py:96
  238.6 3.1 fusion.36
  244.3 3.1 fusion.42
  250.0 3.1 fusion.48
  253.0 13.8 %fusion.57 = f32[8,64,128]{1,0,2:T(8,128)} fusion(bf16[3,64,64,128]{2,1,0,3:T(8,128)(2,1)S(1)} %bitcast.177, pred[3,64,64]{2,1,0:T(8,128)(4,1)S(1)} %fusion.94, bf16[3,8,64,512]{2,1,0,3:T(8,128)(2,1)S(1)} %maximum_bitcast_fusion.1), kind=kOutput, calls=%fused_computation.54 | convolution fusion | flops 26738688 | bytes 7364608 | tf_op jit(solution)/shard_map/knbc,kcba->nac/dot_general | solution.py:96
  266.9 3.1 fusion.54
  275.3 2.6 copy.63
  280.1 5.4 fusion.63
  286.2 5.6 fusion.66
  292.6 5.4 fusion.69
  298.8 5.4 fusion.60
  314.7 242.4 %all-reduce.2.cloned.1.call-done = f32[128,512]{0,1:T(8,128)} async-done(((f32[128,512]{0,1:T(8,128)}), f32[128,512]{0,1:T(8,128)}) %all-reduce.2.cloned.1.call-update) | async-done | bytes 262160 | tf_op jit(solution)/shard_map/psum | solution.py:118
  (114 shorter events, 50.1 us)
Async XLA Ops:
  7.2 13.3 %copy-start.15 = (bf16[128,512]{1,0:T(8,128)(2,1)S(1)}, bf16[128,512]{1,0:T(8,128)(2,1)}, u32[]{:S(2)}) copy-start(bf16[128,512]{1,0:T(8,128)(2,1)} %param.8) | copy-start | bytes 393220
  7.2 550.0 %all-reduce.2.cloned.1.call-start = ((), (), s32[]{:S(2)}) async-start(), calls=%async_computation | async-start | bytes 524288 | tf_op jit(solution)/shard_map/psum | solution.py:118
  8.6 16.9 %copy-start = (bf16[1,512,512]{2,1,0:T(8,128)(2,1)}, bf16[1,512,512]{2,1,0:T(8,128)(2,1)S(1)}, u32[]{:S(2)}) copy-start(bf16[1,512,512]{2,1,0:T(8,128)(2,1)S(1)} %multiply_convert_fusion) | copy-start | bytes 1572868
  9.3 205.5 %collective-permute-start.1 = (bf16[1,127,512]{2,1,0:T(8,128)(2,1)}, bf16[1,127,512]{2,1,0:T(8,128)(2,1)S(1)}, u32[]{:S(2)}, u32[]{:S(2)}) collective-permute-start(bf16[1,127,512]{2,1,0:T(8,128)(2,1)} %slice.196), channel_id=1, source_target_pairs={{8,0},{16,8},{24,16},{32,24},{40,32},{48,40},{56,48},{64,56},{72,6... | collective-permute-start | bytes 390152 | tf_op jit(solution)/shard_map/ppermute | solution.py:12
  17.3 197.5 %collective-permute-start = (bf16[1,127,512]{2,1,0:T(8,128)(2,1)}, bf16[1,127,512]{2,1,0:T(8,128)(2,1)}, u32[]{:S(2)}, u32[]{:S(2)}) collective-permute-start(bf16[1,127,512]{2,1,0:T(8,128)(2,1)} %slice.188), channel_id=1, source_target_pairs={{0,8},{8,16},{16,24},{24,32},{32,40},{40,48},{48,56},{56,64},{64,7... | collective-permute-start | bytes 390152 | tf_op jit(solution)/shard_map/ppermute | solution.py:12
  229.7 2.2 copy-start.3
  232.0 6.7 %slice-start = ((s8[6291456]{0:T(1024)(128)(4,1)}), s8[4194304]{0:T(1024)(128)(4,1)S(1)}, s32[]{:S(2)}) async-start(s8[6291456]{0:T(1024)(128)(4,1)} %bitcast.172), calls=%async_computation.1 | async-start | bytes 8388608
  232.8 5.8 %slice-start.1 = ((s8[6291456]{0:T(1024)(128)(4,1)}), s8[2097152]{0:T(1024)(128)(4,1)S(1)}, s32[]{:S(2)}) async-start(s8[6291456]{0:T(1024)(128)(4,1)} %bitcast.172), calls=%async_computation.2 | async-start | bytes 4194304
  232.8 8.9 %slice-start.2 = ((s8[6291456]{0:T(1024)(128)(4,1)}), s8[4194304]{0:T(1024)(128)(4,1)S(1)}, s32[]{:S(2)}) async-start(s8[6291456]{0:T(1024)(128)(4,1)} %bitcast.174), calls=%async_computation.3 | async-start | bytes 8388608
  238.6 3.1 slice-start.3
  241.7 5.7 %slice-start.6 = ((s8[6291456]{0:T(1024)(128)(4,1)}), s8[4194304]{0:T(1024)(128)(4,1)S(1)}, s32[]{:S(2)}) async-start(s8[6291456]{0:T(1024)(128)(4,1)} %bitcast.178), calls=%async_computation.7 | async-start | bytes 8388608
  244.3 3.1 slice-start.7
  247.4 5.7 slice-start.4
  250.0 3.1 slice-start.5
  280.1 5.4 copy-start.10
  286.2 5.6 copy-start.9
  292.6 5.4 copy-start.8
  298.7 6.2 %copy-start.14 = (f32[8,64,128]{1,0,2:T(8,128)S(1)}, f32[8,64,128]{1,0,2:T(8,128)}, u32[]{:S(2)}) copy-start(f32[8,64,128]{1,0,2:T(8,128)} %fusion.36) | copy-start | bytes 786436
  298.7 6.4 %copy-start.12 = (f32[8,64,128]{1,0,2:T(8,128)S(1)}, f32[8,64,128]{1,0,2:T(8,128)}, u32[]{:S(2)}) copy-start(f32[8,64,128]{1,0,2:T(8,128)} %fusion.39) | copy-start | bytes 786436
  298.7 6.6 %copy-start.13 = (f32[8,64,128]{1,0,2:T(8,128)S(1)}, f32[8,64,128]{1,0,2:T(8,128)}, u32[]{:S(2)}) copy-start(f32[8,64,128]{1,0,2:T(8,128)} %fusion.42) | copy-start | bytes 786436
  298.7 6.8 %copy-start.11 = (f32[8,64,128]{1,0,2:T(8,128)S(1)}, f32[8,64,128]{1,0,2:T(8,128)}, u32[]{:S(2)}) copy-start(f32[8,64,128]{1,0,2:T(8,128)} %fusion.45) | copy-start | bytes 786436
  304.9 6.6 %copy-start.5 = (bf16[1,512,512]{2,1,0:T(8,128)(2,1)S(1)}, bf16[1,512,512]{2,1,0:T(8,128)(2,1)}, u32[]{:S(2)}) copy-start(bf16[1,512,512]{2,1,0:T(8,128)(2,1)} %param.9) | copy-start | bytes 1572868
  305.6 7.0 %copy-start.6 = (bf16[1,512,512]{2,1,0:T(8,128)(2,1)S(1)}, bf16[1,512,512]{2,1,0:T(8,128)(2,1)}, u32[]{:S(2)}) copy-start(bf16[1,512,512]{2,1,0:T(8,128)(2,1)} %param.7) | copy-start | bytes 1572868
  305.6 7.0 %copy-start.7 = (bf16[1,512,512]{2,1,0:T(8,128)(2,1)S(1)}, bf16[1,512,512]{2,1,0:T(8,128)(2,1)}, u32[]{:S(2)}) copy-start(bf16[1,512,512]{2,1,0:T(8,128)(2,1)} %param.6) | copy-start | bytes 1572868
  (3 other events, 5.2 us)
Sparse Core Ops, SparseCore 0:
  305.0 252.1 all-reduce.1
where the time goes:
time: 574 us; the launch traced here: 566 us
  waiting for transfers between devices  242 us (42%)
  local copies, waits for them, and re-layouts  225 us (39%)
  matrix products  63.2 us (11%)
  between operations  14.9 us (3%)
  other arithmetic  12.3 us (2%)
  starting transfers between devices  7.98 us (1%)
    psum x1, waiting for transfers between devices, shards(): lax.psum(jnp.concatenate([filter_part(first) for first in starts], axis=1...  242 us
    gather x8, local copies, waits for them, and re-layouts, block_matrices(): picked = taps_part[jnp.clip(offsets, 0, tap_count - 1)]  189 us
    dot_general x4, matrix products, grad_part(): jnp.einsum('knbc,kcba->nac', stack_after[:, :, :, first_chan:last_chan],...  24.8 us
    dot_general x4, matrix products, filter_part(): jnp.einsum('caw,awj->jc', product, selector, precision=lax.Precision.HIGH...  21.6 us
    unnamed x59, local copies, waits for them, and re-layouts  13.4 us
    dot_general x4, matrix products, grad_part(): jnp.einsum('knbc,kcab->nac', stack_before[:, :, :, first_chan:last_chan],...  12.3 us
  transfers between devices with their start and end apart: 3, of which 1 were waited for; matrix products, arithmetic and copies ran while one was open for 36% of the time, Pallas kernels for 0%

commit v1 on v0

v1 whole, which is shorter than its diff:
```python
import functools
import math

import jax
import jax.numpy as jnp
import ml_dtypes
import numpy as np
from jax import lax
from jax.experimental import pallas as pl
from jax.experimental.pallas import tpu as pltpu
from jax.sharding import Mesh, PartitionSpec as P

F32 = jnp.float32
BF16 = jnp.bfloat16
BLOCK = 128
SPEC = 256
HALF = BLOCK // 2
WIDTH = 256
VMEM_LIMIT = 40 * 1024 * 1024


def split_in_two(matrix):
    high = matrix.astype(ml_dtypes.bfloat16)
    low = (matrix - high.astype(np.float64)).astype(ml_dtypes.bfloat16)
    return high, low


def transform_matrices():
    freqs = np.concatenate([np.arange(0, BLOCK, 2), np.arange(1, BLOCK, 2)])
    angles = 2 * np.pi * freqs[:, None] * np.arange(BLOCK)[None, :] / SPEC
    real, imag = np.cos(angles), -np.sin(angles)
    imag[0] = np.cos(np.pi * np.arange(BLOCK))
    forward = np.concatenate([real, imag], axis=0)
    weight = np.full((SPEC,), 2.0 / SPEC)
    weight[0] = weight[BLOCK] = 1.0 / SPEC
    inverse = (forward * weight[:, None]).T
    return (
        np.concatenate(split_in_two(forward), axis=1),
        np.concatenate(split_in_two(inverse), axis=1),
    )


def dot(left, right):
    return jnp.dot(left, right, preferred_element_type=F32)


def spectrum(forward, block):
    both = dot(forward, jnp.concatenate([block, block], axis=0))
    return both[:BLOCK], both[BLOCK:]


def inverse_of(inverse, real, imag):
    both = jnp.concatenate([real, imag], axis=0)
    high = both.astype(BF16)
    low = (both - high.astype(F32)).astype(BF16)
    return dot(inverse, jnp.concatenate([high, high], axis=0)) + dot(inverse[:, :SPEC], low)


def beside(first, second):
    def joined(a, b):
        return jnp.concatenate([a[:HALF] + b[:HALF], a[HALF:] - b[HALF:]], axis=0)

    return joined(first[0], second[0]), joined(first[1], second[1])


def first_row(shape):
    return lax.broadcasted_iota(jnp.int32, shape, 0) == 0


def product(left, right):
    return (left.astype(F32) * right.astype(F32)).astype(BF16)


def rows(ref, block):
    return ref[0, pl.ds(block * BLOCK, BLOCK), :]


def correlation_terms(grad, gated):
    real = grad[0] * gated[0]
    imag = grad[1] * gated[1]
    cross = grad[1] * gated[0] - grad[0] * gated[1]
    return real, imag, cross


def correlation(inverse, terms):
    real, imag, cross = terms
    top = first_row(real.shape)
    return inverse_of(
        inverse, real + jnp.where(top, 0.0, imag), jnp.where(top, imag, cross)
    )


def edge_kernel(key_ref, value_ref, query_ref, grad_ref, gated_ref, mix_ref):
    gated_ref[...] = product(key_ref[0], value_ref[0])
    mix_ref[...] = product(query_ref[0], grad_ref[0])


def inner_kernel(query_ref, key_ref, value_ref, grad_ref, fwd_ref, inv_ref, out_ref):
    fwd = fwd_ref[...]
    blocks = query_ref.shape[1] // BLOCK
    terms = None
    before = None
    for n in range(blocks):
        gated = spectrum(fwd, product(rows(key_ref, n), rows(value_ref, n)))
        grad = spectrum(fwd, product(rows(query_ref, n), rows(grad_ref, n)))
        window = gated if before is None else beside(gated, before)
        more = correlation_terms(grad, window)
        terms = more if terms is None else tuple(a + b for a, b in zip(terms, more))
        before = gated
    out_ref[...] = correlation(inv_ref[...], terms)


def outer_kernel(halo_ref, mix_ref, inner_ref, fwd_ref, inv_ref, out_ref):
    fwd = fwd_ref[...]
    halo = spectrum(fwd, halo_ref[...])
    zero = jnp.zeros_like(halo[0])
    window = beside((zero, zero), halo)
    grad = spectrum(fwd, mix_ref[...])
    total = inner_ref[...] + correlation(inv_ref[...], correlation_terms(grad, window))
    for part in range(total.shape[1] // 128):
        out_ref[pl.ds(part * BLOCK, BLOCK), :] = total[:, part * 128 : (part + 1) * 128].astype(BF16)


def conv_kernel(
    query_ref, key_ref, value_ref, grad_ref, before_ref, after_ref, taps_ref, fwd_ref, inv_ref,
    out_query_ref, out_key_ref, out_value_ref,
):
    fwd, inv = fwd_ref[...], inv_ref[...]
    blocks = query_ref.shape[1] // BLOCK
    real, imag = spectrum(fwd, taps_ref[...])
    top = first_row(real.shape)
    cross = jnp.where(top, 0.0, imag)
    last = jnp.where(top, imag, real)
    before = spectrum(fwd, before_ref[...])
    for n in range(blocks):
        gated = spectrum(fwd, product(rows(key_ref, n), rows(value_ref, n)))
        wr, wi = beside(gated, before)
        mixed = inverse_of(inv, wr * real - wi * cross, wr * cross + wi * last)
        out_query_ref[0, pl.ds(n * BLOCK, BLOCK), :] = (
            rows(grad_ref, n).astype(F32) * mixed
        ).astype(BF16)
        before = gated
    after = spectrum(fwd, after_ref[...])
    for n in reversed(range(blocks)):
        grad = spectrum(fwd, product(rows(query_ref, n), rows(grad_ref, n)))
        wr, wi = beside(grad, after)
        carried = inverse_of(inv, wr * real + wi * cross, wi * last - wr * cross)
        out_key_ref[0, pl.ds(n * BLOCK, BLOCK), :] = (
            carried * rows(value_ref, n).astype(F32)
        ).astype(BF16)
        out_value_ref[0, pl.ds(n * BLOCK, BLOCK), :] = (
            carried * rows(key_ref, n).astype(F32)
        ).astype(BF16)
        after = grad


def params():
    return pltpu.CompilerParams(vmem_limit_bytes=VMEM_LIMIT)


def cost(flops, moved):
    return pl.CostEstimate(flops=flops, bytes_accessed=moved, transcendentals=0)


def shards(query_act, key_act, value_act, filter_taps, grad_out, count_all=1):
    _, row_count, chan_count = query_act.shape
    blocks = row_count // BLOCK
    steps = chan_count // WIDTH
    fwd_np, inv_np = transform_matrices()
    fwd, inv = jnp.asarray(fwd_np), jnp.asarray(inv_np)

    whole = pl.BlockSpec((1, row_count, WIDTH), lambda i: (0, 0, i))
    slab = pl.BlockSpec((BLOCK, WIDTH), lambda i: (0, i))
    fwd_spec = pl.BlockSpec(fwd.shape, lambda i: (0, 0))
    inv_spec = pl.BlockSpec(inv.shape, lambda i: (0, 0))

    last_rows = pl.BlockSpec((1, BLOCK, chan_count), lambda i: (0, blocks - 1, 0))
    first_rows = pl.BlockSpec((1, BLOCK, chan_count), lambda i: (0, 0, 0))
    edge = pl.BlockSpec((BLOCK, chan_count), lambda i: (0, 0))
    edge_shape = jax.ShapeDtypeStruct((BLOCK, chan_count), BF16)
    gated_edge, mix_edge = pl.pallas_call(
        edge_kernel,
        grid=(1,),
        in_specs=[last_rows, last_rows, first_rows, first_rows],
        out_specs=[edge, edge],
        out_shape=[edge_shape, edge_shape],
        compiler_params=params(),
        cost_estimate=cost(200_000, 800_000),
        name="edges",
    )(key_act, value_act, query_act, grad_out)

    ctx = ("z", "xh", "c")
    ring = 1
    for name in ctx:
        ring *= lax.axis_size(name)
    before = lax.ppermute(gated_edge, ctx, [(i, i + 1) for i in range(ring - 1)])
    after = lax.ppermute(mix_edge, ctx, [(i + 1, i) for i in range(ring - 1)])

    inner = pl.pallas_call(
        inner_kernel,
        grid=(steps,),
        in_specs=[whole, whole, whole, whole, fwd_spec, inv_spec],
        out_specs=slab,
        out_shape=jax.ShapeDtypeStruct((BLOCK, chan_count), F32),
        compiler_params=params(),
        cost_estimate=cost(800_000_000, 2_500_000),
        name="inner_pairs",
    )(query_act, key_act, value_act, grad_out, fwd, inv)

    partial = pl.pallas_call(
        outer_kernel,
        grid=(steps,),
        in_specs=[slab, slab, slab, fwd_spec, inv_spec],
        out_specs=pl.BlockSpec((BLOCK * WIDTH // 128, 128), lambda i: (i, 0)),
        out_shape=jax.ShapeDtypeStruct((BLOCK * chan_count // 128, 128), BF16),
        compiler_params=params(),
        cost_estimate=cost(200_000_000, 800_000),
        name="outer_pairs",
    )(before, mix_edge, inner, fwd, inv)

    near = ("xh", "c", "y", "xl")
    near_count = 1
    for name in near:
        near_count *= lax.axis_size(name)
    far = "z"
    far_count = lax.axis_size(far)
    chunks = partial.reshape(near_count, -1, 128)
    mine = lax.all_to_all(chunks, near, 0, 0, tiled=True).astype(F32).sum(axis=0)
    planes = jnp.broadcast_to(mine[None], (far_count,) + mine.shape)
    mine = lax.all_to_all(planes, far, 0, 0, tiled=True).sum(axis=0) / math.sqrt(count_all)
    copies = jnp.broadcast_to(mine.astype(BF16)[None], (near_count,) + mine.shape)
    total = lax.all_to_all(copies, near, 0, 0, tiled=True)
    total = total.reshape(chan_count // 128, BLOCK, 128).astype(F32)
    grad_filter = jnp.concatenate([total[i] for i in range(chan_count // 128)], axis=1)

    out_shape = jax.ShapeDtypeStruct(query_act.shape, BF16)
    grad_query, grad_key, grad_value = pl.pallas_call(
        conv_kernel,
        grid=(steps,),
        in_specs=[whole, whole, whole, whole, slab, slab, slab, fwd_spec, inv_spec],
        out_specs=[whole, whole, whole],
        out_shape=[out_shape, out_shape, out_shape],
        compiler_params=params(),
        cost_estimate=cost(2_000_000_000, 4_000_000),
        name="convolutions",
    )(query_act, key_act, value_act, grad_out, before, after, filter_taps, fwd, inv)
    return grad_query, grad_key, grad_value, grad_filter


def solution(mesh):
    fine = Mesh(mesh.devices.reshape(8, 2, 2, 4, 2), ("z", "xh", "c", "y", "xl"))
    spec = P(("y", "xl"), ("z", "xh", "c"), None)

    def whole(query_act, key_act, value_act, filter_taps, grad_out):
        count_all = query_act.shape[0] * query_act.shape[1]
        return jax.shard_map(
            functools.partial(shards, count_all=count_all),
            mesh=fine,
            in_specs=(spec, spec, spec, P(), spec),
            out_specs=(spec, spec, spec, P()),
            check_vma=False,
        )(query_act, key_act, value_act, filter_taps, grad_out)

    return whole
```

time: 574 us -> 62 us (0.11); the launches traced: 566 us -> 61.5 us
  waiting for transfers between devices: 242 us -> 8.26 us
  local copies, waits for them, and re-layouts: 225 us -> 5.52 us
  matrix products: 63.2 us -> 0 us
  blocking collectives: 0 us -> 16.1 us
  starting transfers between devices: 7.98 us -> 22.9 us
  between operations: 14.9 us -> 0.79 us
  other arithmetic: 12.3 us -> 0.77 us
  Pallas kernels: 0 us -> 7.24 us
    psum x1 -> x0, waiting for transfers between devices: 242 us -> none  [shards(): lax.psum(jnp.concatenate([filter_part(first) for first in starts], axis=1...]
    gather x8 -> x0, local copies, waits for them, and re-layouts: 189 us -> none  [block_matrices(): picked = taps_part[jnp.clip(offsets, 0, tap_count - 1)]]
    dot_general x16 -> x0, matrix products: 63.2 us -> none  [the longest x4 24.8 us: grad_part(): jnp.einsum('knbc,kcba->nac', stack_after[:, :, :, first_chan:last_chan],...]
    slice x15 -> x1, local copies, waits for them, and re-layouts: 16.1 us -> 0.02 us  [shards(): total[i]]
    all_to_all x0 -> x1, blocking collectives: none -> 16.1 us  [shards(): lax.all_to_all(chunks, near, 0, 0, tiled=True).astype(F32).sum(axis=0)]
    all_to_all x0 -> x2, starting transfers between devices: none -> 14.1 us  [the longest x1 8.76 us: shards(): lax.all_to_all(planes, far, 0, 0, tiled=True).sum(axis=0)]
    unnamed x59 -> x22, local copies, waits for them, and re-layouts: 13.4 us -> 4.19 us
    all_to_all x0 -> x2, waiting for transfers between devices: none -> 8.16 us  [the longest x1 4.66 us: shards(): lax.all_to_all(planes, far, 0, 0, tiled=True).sum(axis=0)]
  transfers between devices with their start and end apart: 3 -> 4, of which waited for: 1 -> 3; matrix products, arithmetic and copies ran while one was open for 36% -> 1% of each run, Pallas kernels for 0% -> 10%
where the time goes in v1:
time: 62 us; the launch traced here: 61.5 us
  starting transfers between devices  22.9 us (37%)
  blocking collectives  16.1 us (26%)
  waiting for transfers between devices  8.26 us (13%)
  Pallas kernels  7.24 us (12%)
  local copies, waits for them, and re-layouts  5.52 us (9%)
  between operations  0.79 us (1%)
  other arithmetic  0.77 us (1%)
    all_to_all x1, blocking collectives, shards(): lax.all_to_all(chunks, near, 0, 0, tiled=True).astype(F32).sum(axis=0)  16.1 us
    all_to_all x1, starting transfers between devices, shards(): lax.all_to_all(planes, far, 0, 0, tiled=True).sum(axis=0)  8.76 us
    ppermute x1, starting transfers between devices, shards(): lax.ppermute(gated_edge, ctx, [(i, i + 1) for i in range(ring - 1)])  6.17 us
    all_to_all x1, starting transfers between devices, shards(): total = lax.all_to_all(copies, near, 0, 0, tiled=True)  5.37 us
    all_to_all x1, waiting for transfers between devices, shards(): lax.all_to_all(planes, far, 0, 0, tiled=True).sum(axis=0)  4.66 us
    pallas_call x1, Pallas kernels, shards(): pl.pallas_call(conv_kernel, grid=(steps,), in_specs=[whole, whole, whole,...  4.23 us
    unnamed x22, local copies, waits for them, and re-layouts  4.19 us
    all_to_all x1, waiting for transfers between devices, shards(): total = lax.all_to_all(copies, near, 0, 0, tiled=True)  3.5 us
  transfers between devices with their start and end apart: 4, of which 3 were waited for; matrix products, arithmetic and copies ran while one was open for 1% of the time, Pallas kernels for 10%

profile of v1, /device:TPU:1, one launch (start us, length us, event | category | flops | bytes accessed | tf_op | source)
XLA Modules:
  0.0 61.5 jit_solution(18258523584576723470)
XLA Ops:
  0.6 0.0 copy-start
  0.6 1.0 %copy-done = bf16[1,512,512]{2,1,0:T(8,128)(2,1)S(1)} copy-done((bf16[1,512,512]{2,1,0:T(8,128)(2,1)S(1)}, bf16[1,512,512]{2,1,0:T(8,128)(2,1)}, u32[]{:S(2)}) %copy-start) | copy-done | bytes 524312
  1.7 1.0 %copy-done.2 = bf16[1,512,512]{2,1,0:T(8,128)(2,1)S(1)} copy-done((bf16[1,512,512]{2,1,0:T(8,128)(2,1)S(1)}, bf16[1,512,512]{2,1,0:T(8,128)(2,1)}, u32[]{:S(2)}) %copy-start.2) | copy-done | bytes 524312
  2.7 1.0 %copy-done.4 = bf16[1,512,512]{2,1,0:T(8,128)(2,1)S(1)} copy-done((bf16[1,512,512]{2,1,0:T(8,128)(2,1)S(1)}, bf16[1,512,512]{2,1,0:T(8,128)(2,1)}, u32[]{:S(2)}) %copy-start.4) | copy-done | bytes 524312
  3.8 1.0 %copy-done.6 = bf16[1,512,512]{2,1,0:T(8,128)(2,1)S(1)} copy-done((bf16[1,512,512]{2,1,0:T(8,128)(2,1)S(1)}, bf16[1,512,512]{2,1,0:T(8,128)(2,1)}, u32[]{:S(2)}) %copy-start.6) | copy-done | bytes 524312
  4.8 0.1 edges.1
  4.9 6.2 %collective-permute-start = (bf16[128,512]{1,0:T(8,128)(2,1)S(1)}, bf16[128,512]{1,0:T(8,128)(2,1)S(1)}, u32[]{:S(2)}, u32[]{:S(2)}) collective-permute-start(bf16[128,512]{1,0:T(8,128)(2,1)S(1)} %get-tuple-element.9), channel_id=1, source_target_pairs={{0,8},{8,16},{16,24},{24,32},{32,40},{40,48},{48,56},{56,64},{64,7... | collective-permute-start | bytes 393224 | tf_op jit(solution)/shard_map/ppermute | solution.py:196
  11.1 0.0 copy-start.7
  11.1 1.8 %inner_pairs.1.inner_ref = f32[128,512]{1,0:T(8,128)S(1)} custom-call(bf16[1,512,512]{2,1,0:T(8,128)(2,1)S(1)} %copy-done, bf16[1,512,512]{2,1,0:T(8,128)(2,1)S(1)} %copy-done.2, bf16[1,512,512]{2,1,0:T(8,128)(2,1)S(1)} %copy-done.4, bf16[1,512,512]{2,1,0:T(8,128)(2,1)S(1)} %copy-done.6, bf16[256,256]{1,0:T(8,128)(2,1)S(1)} %copy-done.9, ...), custom_call_target="tpu_custom_call" | custom-call | flops 800000000 | bytes 2500000 | tf_op jit(solution)/shard_map/inner_pairs/pallas_call | solution.py:199
  12.9 0.1 collective-permute-done.before_ref.halo_ref
  13.0 1.2 %outer_pairs.1 = bf16[512,128]{1,0:T(8,128)(2,1)S(1)} custom-call(bf16[128,512]{1,0:T(8,128)(2,1)S(1)} %collective-permute-done.before_ref.halo_ref, bf16[128,512]{1,0:T(8,128)(2,1)S(1)} %get-tuple-element.10.mix_ref, f32[128,512]{1,0:T(8,128)S(1)} %inner_pairs.1.inner_ref, bf16[256,256]{1,0:T(8,128)(2,1)S(1)} %copy-done.9, bf16[128,512]{1,0:T(8,128)(2,1)S(1)} %copy-done.8), custom_call_target="tpu_custom_call" | custom-call | flops 200000000 | bytes 800000 | tf_op jit(solution)/shard_map/outer_pairs/pallas_call | solution.py:210
  14.1 0.0 copy-start.1
  14.2 0.0 copy-start.3
  14.2 16.1 %all_to_all.15 = bf16[32,16,128]{2,1,0:T(8,128)(2,1)S(1)} all-to-all(bf16[32,16,128]{2,1,0:T(8,128)(2,1)S(1)} %bitcast.5), channel_id=1, replica_groups=mesh['z'=8,'xh'=2,'c'=2,'y'=4,'xl'=2] {'xh','c','y','xl'}, dimensions={0} | all-to-all | bytes 262144 | tf_op jit(solution)/shard_map/all_to_all | solution.py:228
  30.3 0.6 %broadcast_in_dim.4 = f32[8,16,128]{2,1,0:T(8,128)} broadcast(f32[16,128]{1,0:T(8,128)S(1)} %convert_reduce_fusion), dimensions={1,2} | broadcast | bytes 73728 | tf_op jit(solution)/shard_map/broadcast_in_dim | solution.py:229
  30.9 8.8 %all-to-all-start.1 = ((f32[8,16,128]{2,1,0:T(8,128)}), f32[8,16,128]{2,1,0:T(8,128)S(1)}, u32[]{:S(2)}, u32[]{:S(2)}) async-start(f32[8,16,128]{2,1,0:T(8,128)} %broadcast_in_dim.4), calls=%async_computation.1 | async-start | bytes 131072 | tf_op jit(solution)/shard_map/all_to_all | solution.py:230
  39.7 2.6 %collective-permute-start.1 = (bf16[128,512]{1,0:T(8,128)(2,1)S(1)}, bf16[128,512]{1,0:T(8,128)(2,1)S(1)}, u32[]{:S(2)}, u32[]{:S(2)}) collective-permute-start(bf16[128,512]{1,0:T(8,128)(2,1)S(1)} %get-tuple-element.10.mix_ref), channel_id=1, source_target_pairs={{8,0},{16,8},{24,16},{32,24},{40,32},{48,40},{56,48},{64,56},{72,6... | collective-permute-start | bytes 393224 | tf_op jit(solution)/shard_map/ppermute | solution.py:197
  42.2 4.7 %all-to-all-done.1 = f32[8,16,128]{2,1,0:T(8,128)S(1)} async-done(((f32[8,16,128]{2,1,0:T(8,128)}), f32[8,16,128]{2,1,0:T(8,128)S(1)}, u32[]{:S(2)}, u32[]{:S(2)}) %all-to-all-start.1) | async-done | bytes 65568 | tf_op jit(solution)/shard_map/all_to_all | solution.py:230
  46.9 0.7 %broadcast_in_dim.5 = bf16[32,16,128]{2,1,0:T(8,128)(2,1)} broadcast(bf16[16,128]{1,0:T(8,128)(2,1)S(1)} %multiply_convert_fusion), dimensions={1,2} | broadcast | bytes 135168 | tf_op jit(solution)/shard_map/broadcast_in_dim | solution.py:231
  47.6 5.4 %all-to-all-start.2 = ((bf16[32,16,128]{2,1,0:T(8,128)(2,1)}), bf16[32,16,128]{2,1,0:T(8,128)(2,1)S(1)}, u32[]{:S(2)}, u32[]{:S(2)}) async-start(bf16[32,16,128]{2,1,0:T(8,128)(2,1)} %broadcast_in_dim.5), calls=%async_computation.2 | async-start | bytes 262144 | tf_op jit(solution)/shard_map/all_to_all | solution.py:232
  53.0 0.0 collective-permute-done.1.after_ref
  53.0 4.2 %convolutions.1 = (bf16[1,512,512]{2,1,0:T(8,128)(2,1)}, bf16[1,512,512]{2,1,0:T(8,128)(2,1)}, bf16[1,512,512]{2,1,0:T(8,128)(2,1)}) custom-call(bf16[1,512,512]{2,1,0:T(8,128)(2,1)S(1)} %copy-done.1, bf16[1,512,512]{2,1,0:T(8,128)(2,1)S(1)} %copy-done.3, bf16[1,512,512]{2,1,0:T(8,128)(2,1)S(1)} %copy-done.5, bf16[1,512,512]{2,1,0:T(8,128)(2,1)S(1)} %copy-done.7, ...), custom_call_target="tpu_custom_call" | custom-call | flops 2000000000 | bytes 4000000 | tf_op jit(solution)/shard_map/convolutions/pallas_call | solution.py:237
  57.3 3.5 %all-to-all-done.2 = bf16[32,16,128]{2,1,0:T(8,128)(2,1)S(1)} async-done(((bf16[32,16,128]{2,1,0:T(8,128)(2,1)}), bf16[32,16,128]{2,1,0:T(8,128)(2,1)S(1)}, u32[]{:S(2)}, u32[]{:S(2)}) %all-to-all-start.2) | async-done | bytes 131104 | tf_op jit(solution)/shard_map/all_to_all | solution.py:232
  60.8 0.7 %pad_maximum_fusion = f32[128,512]{1,0:T(8,128)} fusion(f32[128,128]{1,0:T(8,128)S(1)} %bitcast.9, f32[128,128]{1,0:T(8,128)S(1)} %bitcast.8, f32[128,128]{1,0:T(8,128)S(1)} %bitcast.7, f32[128,128]{1,0:T(8,128)S(1)} %bitcast.6), kind=kLoop, calls=%fused_computation | loop fusion | flops 196608 | bytes 524288 | tf_op jit(solution)/shard_map/concatenate | solution.py:234
  (18 shorter events, 0.1 us)
Async XLA Ops:
  0.6 1.0 %copy-start = (bf16[1,512,512]{2,1,0:T(8,128)(2,1)S(1)}, bf16[1,512,512]{2,1,0:T(8,128)(2,1)}, u32[]{:S(2)}) copy-start(bf16[1,512,512]{2,1,0:T(8,128)(2,1)} %query_ref.5) | copy-start | bytes 1572868
  1.7 1.0 %copy-start.2 = (bf16[1,512,512]{2,1,0:T(8,128)(2,1)S(1)}, bf16[1,512,512]{2,1,0:T(8,128)(2,1)}, u32[]{:S(2)}) copy-start(bf16[1,512,512]{2,1,0:T(8,128)(2,1)} %key_ref.5) | copy-start | bytes 1572868
  2.7 1.0 %copy-start.4 = (bf16[1,512,512]{2,1,0:T(8,128)(2,1)S(1)}, bf16[1,512,512]{2,1,0:T(8,128)(2,1)}, u32[]{:S(2)}) copy-start(bf16[1,512,512]{2,1,0:T(8,128)(2,1)} %value_ref.5) | copy-start | bytes 1572868
  3.8 1.0 %copy-start.6 = (bf16[1,512,512]{2,1,0:T(8,128)(2,1)S(1)}, bf16[1,512,512]{2,1,0:T(8,128)(2,1)}, u32[]{:S(2)}) copy-start(bf16[1,512,512]{2,1,0:T(8,128)(2,1)} %grad_ref.5) | copy-start | bytes 1572868
  4.8 6.3 %copy-start.8 = (bf16[128,512]{1,0:T(8,128)(2,1)S(1)}, bf16[128,512]{1,0:T(8,128)(2,1)}, u32[]{:S(2)}) copy-start(bf16[128,512]{1,0:T(8,128)(2,1)} %constant.10.clone.inv_ref) | copy-start | bytes 393220
  4.8 6.3 %copy-start.9 = (bf16[256,256]{1,0:T(8,128)(2,1)S(1)}, bf16[256,256]{1,0:T(8,128)(2,1)}, u32[]{:S(2)}) copy-start(bf16[256,256]{1,0:T(8,128)(2,1)} %constant.9.clone.fwd_ref) | copy-start | bytes 393220
  4.9 8.1 %collective-permute-start = (bf16[128,512]{1,0:T(8,128)(2,1)S(1)}, bf16[128,512]{1,0:T(8,128)(2,1)S(1)}, u32[]{:S(2)}, u32[]{:S(2)}) collective-permute-start(bf16[128,512]{1,0:T(8,128)(2,1)S(1)} %get-tuple-element.9), channel_id=1, source_target_pairs={{0,8},{8,16},{16,24},{24,32},{32,40},{40,48},{48,56},{56,64},{64,7... | collective-permute-start | bytes 393224 | tf_op jit(solution)/shard_map/ppermute | solution.py:196
  11.1 41.9 %copy-start.7 = (bf16[1,512,512]{2,1,0:T(8,128)(2,1)S(1)}, bf16[1,512,512]{2,1,0:T(8,128)(2,1)}, u32[]{:S(2)}) copy-start(bf16[1,512,512]{2,1,0:T(8,128)(2,1)} %grad_ref.5) | copy-start | bytes 1572868
  13.0 40.0 %copy-start.5 = (bf16[1,512,512]{2,1,0:T(8,128)(2,1)S(1)}, bf16[1,512,512]{2,1,0:T(8,128)(2,1)}, u32[]{:S(2)}) copy-start(bf16[1,512,512]{2,1,0:T(8,128)(2,1)} %value_ref.5) | copy-start | bytes 1572868
  13.0 40.0 %copy-start.10 = (bf16[128,512]{1,0:T(8,128)(2,1)S(1)}, bf16[128,512]{1,0:T(8,128)(2,1)}, u32[]{:S(2)}) copy-start(bf16[128,512]{1,0:T(8,128)(2,1)} %taps_ref.1) | copy-start | bytes 393220
  14.1 38.9 %copy-start.1 = (bf16[1,512,512]{2,1,0:T(8,128)(2,1)S(1)}, bf16[1,512,512]{2,1,0:T(8,128)(2,1)}, u32[]{:S(2)}) copy-start(bf16[1,512,512]{2,1,0:T(8,128)(2,1)} %query_ref.5) | copy-start | bytes 1572868
  14.2 38.9 %copy-start.3 = (bf16[1,512,512]{2,1,0:T(8,128)(2,1)S(1)}, bf16[1,512,512]{2,1,0:T(8,128)(2,1)}, u32[]{:S(2)}) copy-start(bf16[1,512,512]{2,1,0:T(8,128)(2,1)} %key_ref.5) | copy-start | bytes 1572868
  30.9 16.0 %all-to-all-start.1 = ((f32[8,16,128]{2,1,0:T(8,128)}), f32[8,16,128]{2,1,0:T(8,128)S(1)}, u32[]{:S(2)}, u32[]{:S(2)}) async-start(f32[8,16,128]{2,1,0:T(8,128)} %broadcast_in_dim.4), calls=%async_computation.1 | async-start | bytes 131072 | tf_op jit(solution)/shard_map/all_to_all | solution.py:230
  39.7 13.3 %collective-permute-start.1 = (bf16[128,512]{1,0:T(8,128)(2,1)S(1)}, bf16[128,512]{1,0:T(8,128)(2,1)S(1)}, u32[]{:S(2)}, u32[]{:S(2)}) collective-permute-start(bf16[128,512]{1,0:T(8,128)(2,1)S(1)} %get-tuple-element.10.mix_ref), channel_id=1, source_target_pairs={{8,0},{16,8},{24,16},{32,24},{40,32},{48,40},{56,48},{64,56},{72,6... | collective-permute-start | bytes 393224 | tf_op jit(solution)/shard_map/ppermute | solution.py:197
  47.6 13.2 %all-to-all-start.2 = ((bf16[32,16,128]{2,1,0:T(8,128)(2,1)}), bf16[32,16,128]{2,1,0:T(8,128)(2,1)S(1)}, u32[]{:S(2)}, u32[]{:S(2)}) async-start(bf16[32,16,128]{2,1,0:T(8,128)(2,1)} %broadcast_in_dim.5), calls=%async_computation.2 | async-start | bytes 262144 | tf_op jit(solution)/shard_map/all_to_all | solution.py:232

commit v2 on v1

--- a/solution.py
+++ b/solution.py
@@ -71,8 +71,8 @@
     return (left.astype(F32) * right.astype(F32)).astype(BF16)
 
 
-def rows(ref, block):
-    return ref[0, pl.ds(block * BLOCK, BLOCK), :]
+def rows(block):
+    return pl.ds(block * BLOCK, BLOCK)
 
 
 def correlation_terms(grad, gated):
@@ -90,19 +90,14 @@
     )
 
 
-def edge_kernel(key_ref, value_ref, query_ref, grad_ref, gated_ref, mix_ref):
-    gated_ref[...] = product(key_ref[0], value_ref[0])
-    mix_ref[...] = product(query_ref[0], grad_ref[0])
-
-
-def inner_kernel(query_ref, key_ref, value_ref, grad_ref, fwd_ref, inv_ref, out_ref):
+def inner_kernel(gated_ref, mix_ref, fwd_ref, inv_ref, out_ref):
     fwd = fwd_ref[...]
-    blocks = query_ref.shape[1] // BLOCK
+    blocks = gated_ref.shape[0] // BLOCK
     terms = None
     before = None
     for n in range(blocks):
-        gated = spectrum(fwd, product(rows(key_ref, n), rows(value_ref, n)))
-        grad = spectrum(fwd, product(rows(query_ref, n), rows(grad_ref, n)))
+        gated = spectrum(fwd, gated_ref[rows(n), :])
+        grad = spectrum(fwd, mix_ref[rows(n), :])
         window = gated if before is None else beside(gated, before)
         more = correlation_terms(grad, window)
         terms = more if terms is None else tuple(a + b for a, b in zip(terms, more))
@@ -122,35 +117,29 @@
 
 
 def conv_kernel(
-    query_ref, key_ref, value_ref, grad_ref, before_ref, after_ref, taps_ref, fwd_ref, inv_ref,
+    gated_ref, mix_ref, key_ref, value_ref, grad_ref, before_ref, after_ref, taps_ref, fwd_ref, inv_ref,
     out_query_ref, out_key_ref, out_value_ref,
 ):
     fwd, inv = fwd_ref[...], inv_ref[...]
-    blocks = query_ref.shape[1] // BLOCK
+    blocks = gated_ref.shape[0] // BLOCK
     real, imag = spectrum(fwd, taps_ref[...])
     top = first_row(real.shape)
     cross = jnp.where(top, 0.0, imag)
     last = jnp.where(top, imag, real)
     before = spectrum(fwd, before_ref[...])
     for n in range(blocks):
-        gated = spectrum(fwd, product(rows(key_ref, n), rows(value_ref, n)))
+        gated = spectrum(fwd, gated_ref[rows(n), :])
         wr, wi = beside(gated, before)
         mixed = inverse_of(inv, wr * real - wi * cross, wr * cross + wi * last)
-        out_query_ref[0, pl.ds(n * BLOCK, BLOCK), :] = (
-            rows(grad_ref, n).astype(F32) * mixed
-        ).astype(BF16)
+        out_query_ref[0, rows(n), :] = (grad_ref[0, rows(n), :].astype(F32) * mixed).astype(BF16)
         before = gated
     after = spectrum(fwd, after_ref[...])
     for n in reversed(range(blocks)):
-        grad = spectrum(fwd, product(rows(query_ref, n), rows(grad_ref, n)))
+        grad = spectrum(fwd, mix_ref[rows(n), :])
         wr, wi = beside(grad, after)
         carried = inverse_of(inv, wr * real + wi * cross, wi * last - wr * cross)
-        out_key_ref[0, pl.ds(n * BLOCK, BLOCK), :] = (
-            carried * rows(value_ref, n).astype(F32)
-        ).astype(BF16)
-        out_value_ref[0, pl.ds(n * BLOCK, BLOCK), :] = (
-            carried * rows(key_ref, n).astype(F32)
-        ).astype(BF16)
+        out_key_ref[0, rows(n), :] = (carried * value_ref[0, rows(n), :].astype(F32)).astype(BF16)
+        out_value_ref[0, rows(n), :] = (carried * key_ref[0, rows(n), :].astype(F32)).astype(BF16)
         after = grad
 
 
@@ -170,42 +159,31 @@
     fwd, inv = jnp.asarray(fwd_np), jnp.asarray(inv_np)
 
     whole = pl.BlockSpec((1, row_count, WIDTH), lambda i: (0, 0, i))
+    stack = pl.BlockSpec((row_count, WIDTH), lambda i: (0, i))
     slab = pl.BlockSpec((BLOCK, WIDTH), lambda i: (0, i))
     fwd_spec = pl.BlockSpec(fwd.shape, lambda i: (0, 0))
     inv_spec = pl.BlockSpec(inv.shape, lambda i: (0, 0))
 
-    last_rows = pl.BlockSpec((1, BLOCK, chan_count), lambda i: (0, blocks - 1, 0))
-    first_rows = pl.BlockSpec((1, BLOCK, chan_count), lambda i: (0, 0, 0))
-    edge = pl.BlockSpec((BLOCK, chan_count), lambda i: (0, 0))
-    edge_shape = jax.ShapeDtypeStruct((BLOCK, chan_count), BF16)
-    gated_edge, mix_edge = pl.pallas_call(
-        edge_kernel,
-        grid=(1,),
-        in_specs=[last_rows, last_rows, first_rows, first_rows],
-        out_specs=[edge, edge],
-        out_shape=[edge_shape, edge_shape],
-        compiler_params=params(),
-        cost_estimate=cost(200_000, 800_000),
-        name="edges",
-    )(key_act, value_act, query_act, grad_out)
+    gated = product(key_act[0], value_act[0])
+    mix = product(query_act[0], grad_out[0])
 
     ctx = ("z", "xh", "c")
     ring = 1
     for name in ctx:
         ring *= lax.axis_size(name)
-    before = lax.ppermute(gated_edge, ctx, [(i, i + 1) for i in range(ring - 1)])
-    after = lax.ppermute(mix_edge, ctx, [(i + 1, i) for i in range(ring - 1)])
+    before = lax.ppermute(gated[row_count - BLOCK :], ctx, [(i, i + 1) for i in range(ring - 1)])
+    after = lax.ppermute(mix[:BLOCK], ctx, [(i + 1, i) for i in range(ring - 1)])
 
     inner = pl.pallas_call(
         inner_kernel,
         grid=(steps,),
-        in_specs=[whole, whole, whole, whole, fwd_spec, inv_spec],
+        in_specs=[stack, stack, fwd_spec, inv_spec],
         out_specs=slab,
         out_shape=jax.ShapeDtypeStruct((BLOCK, chan_count), F32),
         compiler_params=params(),
         cost_estimate=cost(800_000_000, 2_500_000),
         name="inner_pairs",
-    )(query_act, key_act, value_act, grad_out, fwd, inv)
+    )(gated, mix, fwd, inv)
 
     partial = pl.pallas_call(
         outer_kernel,
@@ -216,7 +194,7 @@
         compiler_params=params(),
         cost_estimate=cost(200_000_000, 800_000),
         name="outer_pairs",
-    )(before, mix_edge, inner, fwd, inv)
+    )(before, mix, inner, fwd, inv)
 
     near = ("xh", "c", "y", "xl")
     near_count = 1
@@ -226,6 +204,20 @@
     far_count = lax.axis_size(far)
     chunks = partial.reshape(near_count, -1, 128)
     mine = lax.all_to_all(chunks, near, 0, 0, tiled=True).astype(F32).sum(axis=0)
+    out_shape = jax.ShapeDtypeStruct(query_act.shape, BF16)
+    grad_query, grad_key, grad_value = pl.pallas_call(
+        conv_kernel,
+        grid=(steps,),
+        in_specs=[stack, stack, whole, whole, whole, slab, slab, slab, fwd_spec, inv_spec],
+        out_specs=[whole, whole, whole],
+        out_shape=[out_shape, out_shape, out_shape],
+        compiler_params=params(),
+        cost_estimate=cost(2_000_000_000, 4_000_000),
+        name="convolutions",
+    )(gated, mix, key_act, value_act, grad_out, before, after, filter_taps, fwd, inv)
+    mine, grad_query, grad_key, grad_value = lax.optimization_barrier(
+        (mine, grad_query, grad_key, grad_value)
+    )
     planes = jnp.broadcast_to(mine[None], (far_count,) + mine.shape)
     mine = lax.all_to_all(planes, far, 0, 0, tiled=True).sum(axis=0) / math.sqrt(count_all)
     copies = jnp.broadcast_to(mine.astype(BF16)[None], (near_count,) + mine.shape)
@@ -233,17 +225,6 @@
     total = total.reshape(chan_count // 128, BLOCK, 128).astype(F32)
     grad_filter = jnp.concatenate([total[i] for i in range(chan_count // 128)], axis=1)
 
-    out_shape = jax.ShapeDtypeStruct(query_act.shape, BF16)
-    grad_query, grad_key, grad_value = pl.pallas_call(
-        conv_kernel,
-        grid=(steps,),
-        in_specs=[whole, whole, whole, whole, slab, slab, slab, fwd_spec, inv_spec],
-        out_specs=[whole, whole, whole],
-        out_shape=[out_shape, out_shape, out_shape],
-        compiler_params=params(),
-        cost_estimate=cost(2_000_000_000, 4_000_000),
-        name="convolutions",
-    )(query_act, key_act, value_act, grad_out, before, after, filter_taps, fwd, inv)
     return grad_query, grad_key, grad_value, grad_filter
 
 

time: 62 us -> 59.4 us (0.958)
  blocking collectives: 16.1 us -> 28.7 us
  starting transfers between devices: 22.9 us -> 15.9 us
  local copies, waits for them, and re-layouts: 5.52 us -> 0.1 us
  waiting for transfers between devices: 8.26 us -> 3.4 us
  other arithmetic: 0.77 us -> 2.33 us
    all_to_all x1 -> x2, blocking collectives: 16.1 us -> 28.7 us  [the longest x1 15.8 us: shards(): lax.all_to_all(planes, far, 0, 0, tiled=True).sum(axis=0)]
    all_to_all x2 -> x1, starting transfers between devices: 14.1 us -> 7.82 us  [shards(): lax.all_to_all(chunks, near, 0, 0, tiled=True).astype(F32).sum(axis=0)]
    all_to_all x2 -> x1, waiting for transfers between devices: 8.16 us -> 3.39 us  [shards(): lax.all_to_all(chunks, near, 0, 0, tiled=True).astype(F32).sum(axis=0)]
    unnamed x22 -> x14, local copies, waits for them, and re-layouts: 4.19 us -> 0.04 us
    convert_element_type x0 -> x2, other arithmetic: none -> 1.56 us  [product(): return (left.astype(F32) * right.astype(F32)).astype(BF16)]
    broadcast_in_dim x1, local copies, waits for them, and re-layouts: 0.67 us -> 0.02 us  [shards(): jnp.broadcast_to(mine.astype(BF16)[None], (near_count,) + mine.shape)]
    ppermute x2, starting transfers between devices: 8.74 us -> 8.09 us  [the longest x1 6.04 us: shards(): lax.ppermute(gated[row_count - BLOCK:], ctx, [(i, i + 1) for i in range(r...]
    pallas_call x1, Pallas kernels: 1.16 us -> 1.79 us  [shards(): pl.pallas_call(outer_kernel, grid=(steps,), in_specs=[slab, slab, slab, f...]
  transfers between devices with their start and end apart: 4 -> 3, of which waited for: 3 -> 1; matrix products, arithmetic and copies ran while one was open for 1% -> 0% of each run, Pallas kernels for 10% -> 13%
where the time goes in v2:
time: 59.4 us; the launch traced here: 59.1 us
  blocking collectives  28.7 us (48%)
  starting transfers between devices  15.9 us (27%)
  Pallas kernels  7.76 us (13%)
  waiting for transfers between devices  3.4 us (6%)
  other arithmetic  2.33 us (4%)
  between operations  0.84 us (1%)
    all_to_all x1, blocking collectives, shards(): lax.all_to_all(planes, far, 0, 0, tiled=True).sum(axis=0)  15.8 us
    all_to_all x1, blocking collectives, shards(): total = lax.all_to_all(copies, near, 0, 0, tiled=True)  12.9 us
    all_to_all x1, starting transfers between devices, shards(): lax.all_to_all(chunks, near, 0, 0, tiled=True).astype(F32).sum(axis=0)  7.82 us
    ppermute x1, starting transfers between devices, shards(): lax.ppermute(gated[row_count - BLOCK:], ctx, [(i, i + 1) for i in range(r...  6.04 us
    pallas_call x1, Pallas kernels, shards(): pl.pallas_call(conv_kernel, grid=(steps,), in_specs=[stack, stack, whole,...  4.28 us
    all_to_all x1, waiting for transfers between devices, shards(): lax.all_to_all(chunks, near, 0, 0, tiled=True).astype(F32).sum(axis=0)  3.39 us
    ppermute x1, starting transfers between devices, shards(): lax.ppermute(mix[:BLOCK], ctx, [(i + 1, i) for i in range(ring - 1)])  2.05 us
    pallas_call x1, Pallas kernels, shards(): pl.pallas_call(outer_kernel, grid=(steps,), in_specs=[slab, slab, slab, f...  1.79 us
  transfers between devices with their start and end apart: 3, of which 1 were waited for; matrix products, arithmetic and copies ran while one was open for 0% of the time, Pallas kernels for 13%

profile of v2, /device:TPU:1, one launch (start us, length us, event | category | flops | bytes accessed | tf_op | source)
XLA Modules:
  0.0 59.1 jit_solution(783621135282789373)
XLA Ops:
  0.6 0.0 copy-start.2
  0.6 0.0 copy-start.6
  0.7 1.4 %multiply_convert_fusion.1 = bf16[1,512,512]{2,1,0:T(8,128)(2,1)S(1)} fusion(bf16[1,512,512]{2,1,0:T(8,128)(2,1)} %value_ref.1, bf16[1,512,512]{2,1,0:T(8,128)(2,1)} %key_ref.1), kind=kLoop, calls=%fused_computation.1 | loop fusion | flops 1048576 | bytes 1572864 | tf_op jit(solution)/shard_map/convert_element_type | solution.py:71
  2.1 6.0 %collective-permute-start = (bf16[128,512]{1,0:T(8,128)(2,1)S(1)}, bf16[128,512]{1,0:T(8,128)(2,1)S(1)}, u32[]{:S(2)}, u32[]{:S(2)}) collective-permute-start(bf16[128,512]{1,0:T(8,128)(2,1)S(1)} %slice_bitcast_fusion.1), channel_id=1, source_target_pairs={{0,8},{8,16},{16,24},{24,32},{32,40},{40,48},{48,56},{56,64},{64,7... | collective-permute-start | bytes 393224 | tf_op jit(solution)/shard_map/ppermute | solution.py:174
  8.1 0.0 copy-done.2
  8.2 0.0 copy-done.6
  8.2 0.1 multiply_convert_fusion
  8.3 0.0 copy-start.3
  8.3 0.0 copy-start.4
  8.3 2.1 %collective-permute-start.1 = (bf16[128,512]{1,0:T(8,128)(2,1)S(1)}, bf16[128,512]{1,0:T(8,128)(2,1)S(1)}, u32[]{:S(2)}, u32[]{:S(2)}) collective-permute-start(bf16[128,512]{1,0:T(8,128)(2,1)S(1)} %slice_bitcast_fusion), channel_id=1, source_target_pairs={{8,0},{16,8},{24,16},{32,24},{40,32},{48,40},{56,48},{64,56},{72,6... | collective-permute-start | bytes 393224 | tf_op jit(solution)/shard_map/ppermute | solution.py:175
  10.4 0.0 copy-done.3
  10.4 0.0 copy-done.4
  10.4 1.7 %inner_pairs.1.inner_ref = f32[128,512]{1,0:T(8,128)S(1)} custom-call(bf16[512,512]{1,0:T(8,128)(2,1)S(1)} %bitcast.14, bf16[512,512]{1,0:T(8,128)(2,1)S(1)} %bitcast.11, bf16[256,256]{1,0:T(8,128)(2,1)S(1)} %copy-done.4, bf16[128,512]{1,0:T(8,128)(2,1)S(1)} %copy-done.3), custom_call_target="tpu_custom_call" | custom-call | flops 800000000 | bytes 2500000 | tf_op jit(solution)/shard_map/inner_pairs/pallas_call | solution.py:177
  12.1 0.0 copy-start
  12.1 0.0 copy-start.1
  12.1 0.0 collective-permute-done.halo_ref.before_ref
  12.2 1.8 %outer_pairs.1 = bf16[512,128]{1,0:T(8,128)(2,1)} custom-call(bf16[128,512]{1,0:T(8,128)(2,1)S(1)} %collective-permute-done.halo_ref.before_ref, bf16[512,512]{1,0:T(8,128)(2,1)S(1)} %bitcast.12, f32[128,512]{1,0:T(8,128)S(1)} %inner_pairs.1.inner_ref, bf16[256,256]{1,0:T(8,128)(2,1)S(1)} %copy-done.4, bf16[128,512]{1,0:T(8,128)(2,1)S(1)} %copy-done.3), custom_call_target="tpu_custom_call" | custom-call | flops 200000000 | bytes 800000 | tf_op jit(solution)/shard_map/outer_pairs/pallas_call | solution.py:188
  13.9 7.8 %all-to-all-start = ((bf16[32,16,128]{2,1,0:T(8,128)(2,1)}), bf16[32,16,128]{2,1,0:T(8,128)(2,1)S(1)}, u32[]{:S(2)}, u32[]{:S(2)}) async-start(bf16[32,16,128]{2,1,0:T(8,128)(2,1)} %bitcast.3), calls=%async_computation | async-start | bytes 262144 | tf_op jit(solution)/shard_map/all_to_all | solution.py:206
  21.8 0.0 collective-permute-done.1.after_ref
  21.8 4.3 %convolutions.1 = (bf16[1,512,512]{2,1,0:T(8,128)(2,1)}, bf16[1,512,512]{2,1,0:T(8,128)(2,1)}, bf16[1,512,512]{2,1,0:T(8,128)(2,1)}) custom-call(bf16[512,512]{1,0:T(8,128)(2,1)S(1)} %bitcast.15, bf16[512,512]{1,0:T(8,128)(2,1)S(1)} %bitcast.13, bf16[1,512,512]{2,1,0:T(8,128)(2,1)S(1)} %copy-done.1, bf16[1,512,512]{2,1,0:T(8,128)(2,1)S(1)} %copy-done, ...), custom_call_target="tpu_custom_call" | custom-call | flops 2000000000 | bytes 4000000 | tf_op jit(solution)/shard_map/convolutions/pallas_call | solution.py:208
  26.1 3.4 %all-to-all-done = bf16[32,16,128]{2,1,0:T(8,128)(2,1)S(1)} async-done(((bf16[32,16,128]{2,1,0:T(8,128)(2,1)}), bf16[32,16,128]{2,1,0:T(8,128)(2,1)S(1)}, u32[]{:S(2)}, u32[]{:S(2)}) %all-to-all-start) | async-done | bytes 131104 | tf_op jit(solution)/shard_map/all_to_all | solution.py:206
  29.6 15.8 %all_to_all.15 = f32[8,16,128]{2,1,0:T(8,128)S(1)} all-to-all(f32[8,16,128]{2,1,0:T(8,128)S(1)} %broadcast_in_dim.4), channel_id=1, replica_groups=mesh['z'=8,'xh'=2,'c'=2,'y'=4,'xl'=2] {'z'}, dimensions={0} | all-to-all | bytes 131072 | tf_op jit(solution)/shard_map/all_to_all | solution.py:222
  45.4 12.9 %all_to_all.16 = bf16[32,16,128]{2,1,0:T(8,128)(2,1)S(1)} all-to-all(bf16[32,16,128]{2,1,0:T(8,128)(2,1)S(1)} %broadcast_in_dim.5), channel_id=1, replica_groups=mesh['z'=8,'xh'=2,'c'=2,'y'=4,'xl'=2] {'xh','c','y','xl'}, dimensions={0} | all-to-all | bytes 262144 | tf_op jit(solution)/shard_map/all_to_all | solution.py:224
  58.4 0.7 %pad_maximum_fusion = f32[128,512]{1,0:T(8,128)} fusion(f32[128,128]{1,0:T(8,128)S(1)} %bitcast.19, f32[128,128]{1,0:T(8,128)S(1)} %bitcast.18, f32[128,128]{1,0:T(8,128)S(1)} %bitcast.17, f32[128,128]{1,0:T(8,128)S(1)} %bitcast.16), kind=kLoop, calls=%fused_computation.2 | loop fusion | flops 196608 | bytes 524288 | tf_op jit(solution)/shard_map/concatenate | solution.py:226
  (12 shorter events, 0.1 us)
Async XLA Ops:
  0.6 7.5 %copy-start.2 = (bf16[1,512,512]{2,1,0:T(8,128)(2,1)S(1)}, bf16[1,512,512]{2,1,0:T(8,128)(2,1)}, u32[]{:S(2)}) copy-start(bf16[1,512,512]{2,1,0:T(8,128)(2,1)} %grad_ref.1) | copy-start | bytes 1572868
  0.6 7.5 %copy-start.6 = (bf16[1,512,512]{2,1,0:T(8,128)(2,1)S(1)}, bf16[1,512,512]{2,1,0:T(8,128)(2,1)}, u32[]{:S(2)}) copy-start(bf16[1,512,512]{2,1,0:T(8,128)(2,1)} %param.7) | copy-start | bytes 1572868
  2.1 10.1 %collective-permute-start = (bf16[128,512]{1,0:T(8,128)(2,1)S(1)}, bf16[128,512]{1,0:T(8,128)(2,1)S(1)}, u32[]{:S(2)}, u32[]{:S(2)}) collective-permute-start(bf16[128,512]{1,0:T(8,128)(2,1)S(1)} %slice_bitcast_fusion.1), channel_id=1, source_target_pairs={{0,8},{8,16},{16,24},{24,32},{32,40},{40,48},{48,56},{56,64},{64,7... | collective-permute-start | bytes 393224 | tf_op jit(solution)/shard_map/ppermute | solution.py:174
  8.3 2.1 %copy-start.3 = (bf16[128,512]{1,0:T(8,128)(2,1)S(1)}, bf16[128,512]{1,0:T(8,128)(2,1)}, u32[]{:S(2)}) copy-start(bf16[128,512]{1,0:T(8,128)(2,1)} %constant.10.clone.inv_ref) | copy-start | bytes 393220
  8.3 2.1 %copy-start.4 = (bf16[256,256]{1,0:T(8,128)(2,1)S(1)}, bf16[256,256]{1,0:T(8,128)(2,1)}, u32[]{:S(2)}) copy-start(bf16[256,256]{1,0:T(8,128)(2,1)} %constant.9.clone.fwd_ref) | copy-start | bytes 393220
  8.3 13.4 %collective-permute-start.1 = (bf16[128,512]{1,0:T(8,128)(2,1)S(1)}, bf16[128,512]{1,0:T(8,128)(2,1)S(1)}, u32[]{:S(2)}, u32[]{:S(2)}) collective-permute-start(bf16[128,512]{1,0:T(8,128)(2,1)S(1)} %slice_bitcast_fusion), channel_id=1, source_target_pairs={{8,0},{16,8},{24,16},{32,24},{40,32},{48,40},{56,48},{64,56},{72,6... | collective-permute-start | bytes 393224 | tf_op jit(solution)/shard_map/ppermute | solution.py:175
  12.1 9.7 %copy-start = (bf16[1,512,512]{2,1,0:T(8,128)(2,1)S(1)}, bf16[1,512,512]{2,1,0:T(8,128)(2,1)}, u32[]{:S(2)}) copy-start(bf16[1,512,512]{2,1,0:T(8,128)(2,1)} %value_ref.1) | copy-start | bytes 1572868
  12.1 9.7 %copy-start.1 = (bf16[1,512,512]{2,1,0:T(8,128)(2,1)S(1)}, bf16[1,512,512]{2,1,0:T(8,128)(2,1)}, u32[]{:S(2)}) copy-start(bf16[1,512,512]{2,1,0:T(8,128)(2,1)} %key_ref.1) | copy-start | bytes 1572868
  13.9 7.9 %copy-start.5 = (bf16[128,512]{1,0:T(8,128)(2,1)S(1)}, bf16[128,512]{1,0:T(8,128)(2,1)}, u32[]{:S(2)}) copy-start(bf16[128,512]{1,0:T(8,128)(2,1)} %taps_ref.1) | copy-start | bytes 393220
  13.9 15.6 %all-to-all-start = ((bf16[32,16,128]{2,1,0:T(8,128)(2,1)}), bf16[32,16,128]{2,1,0:T(8,128)(2,1)S(1)}, u32[]{:S(2)}, u32[]{:S(2)}) async-start(bf16[32,16,128]{2,1,0:T(8,128)(2,1)} %bitcast.3), calls=%async_computation | async-start | bytes 262144 | tf_op jit(solution)/shard_map/all_to_all | solution.py:206

commit v3 on v2

--- a/solution.py
+++ b/solution.py
@@ -36,7 +36,7 @@
     inverse = (forward * weight[:, None]).T
     return (
         np.concatenate(split_in_two(forward), axis=1),
-        np.concatenate(split_in_two(inverse), axis=1),
+        np.concatenate(split_in_two(inverse), axis=0),
     )
 
 
@@ -53,7 +53,8 @@
     both = jnp.concatenate([real, imag], axis=0)
     high = both.astype(BF16)
     low = (both - high.astype(F32)).astype(BF16)
-    return dot(inverse, jnp.concatenate([high, high], axis=0)) + dot(inverse[:, :SPEC], low)
+    terms = dot(inverse, high)
+    return terms[:BLOCK] + terms[BLOCK:] + dot(inverse[:BLOCK], low)
 
 
 def beside(first, second):
@@ -91,29 +92,35 @@
 
 
 def inner_kernel(gated_ref, mix_ref, fwd_ref, inv_ref, out_ref):
-    fwd = fwd_ref[...]
+    fwd, inv = fwd_ref[...], inv_ref[...]
     blocks = gated_ref.shape[0] // BLOCK
-    terms = None
-    before = None
-    for n in range(blocks):
-        gated = spectrum(fwd, gated_ref[rows(n), :])
-        grad = spectrum(fwd, mix_ref[rows(n), :])
-        window = gated if before is None else beside(gated, before)
-        more = correlation_terms(grad, window)
-        terms = more if terms is None else tuple(a + b for a, b in zip(terms, more))
-        before = gated
-    out_ref[...] = correlation(inv_ref[...], terms)
+    for part in range(gated_ref.shape[1] // WIDTH):
+        chans = pl.ds(part * WIDTH, WIDTH)
+        terms = None
+        before = None
+        for n in range(blocks):
+            gated = spectrum(fwd, gated_ref[rows(n), chans])
+            grad = spectrum(fwd, mix_ref[rows(n), chans])
+            window = gated if before is None else beside(gated, before)
+            more = correlation_terms(grad, window)
+            terms = more if terms is None else tuple(a + b for a, b in zip(terms, more))
+            before = gated
+        out_ref[:, chans] = correlation(inv, terms)
 
 
 def outer_kernel(halo_ref, mix_ref, inner_ref, fwd_ref, inv_ref, out_ref):
-    fwd = fwd_ref[...]
-    halo = spectrum(fwd, halo_ref[...])
-    zero = jnp.zeros_like(halo[0])
-    window = beside((zero, zero), halo)
-    grad = spectrum(fwd, mix_ref[...])
-    total = inner_ref[...] + correlation(inv_ref[...], correlation_terms(grad, window))
-    for part in range(total.shape[1] // 128):
-        out_ref[pl.ds(part * BLOCK, BLOCK), :] = total[:, part * 128 : (part + 1) * 128].astype(BF16)
+    fwd, inv = fwd_ref[...], inv_ref[...]
+    for part in range(halo_ref.shape[1] // WIDTH):
+        chans = pl.ds(part * WIDTH, WIDTH)
+        halo = spectrum(fwd, halo_ref[:, chans])
+        zero = jnp.zeros_like(halo[0])
+        window = beside((zero, zero), halo)
+        grad = spectrum(fwd, mix_ref[:, chans])
+        total = inner_ref[:, chans] + correlation(inv, correlation_terms(grad, window))
+        for piece in range(WIDTH // 128):
+            out_ref[rows(part * (WIDTH // 128) + piece), :] = total[
+                :, piece * 128 : (piece + 1) * 128
+            ].astype(BF16)
 
 
 def conv_kernel(
@@ -126,21 +133,25 @@
     top = first_row(real.shape)
     cross = jnp.where(top, 0.0, imag)
     last = jnp.where(top, imag, real)
-    before = spectrum(fwd, before_ref[...])
-    for n in range(blocks):
-        gated = spectrum(fwd, gated_ref[rows(n), :])
-        wr, wi = beside(gated, before)
-        mixed = inverse_of(inv, wr * real - wi * cross, wr * cross + wi * last)
-        out_query_ref[0, rows(n), :] = (grad_ref[0, rows(n), :].astype(F32) * mixed).astype(BF16)
-        before = gated
-    after = spectrum(fwd, after_ref[...])
-    for n in reversed(range(blocks)):
-        grad = spectrum(fwd, mix_ref[rows(n), :])
+
+    def backward(n, grad, after):
         wr, wi = beside(grad, after)
         carried = inverse_of(inv, wr * real + wi * cross, wi * last - wr * cross)
         out_key_ref[0, rows(n), :] = (carried * value_ref[0, rows(n), :].astype(F32)).astype(BF16)
         out_value_ref[0, rows(n), :] = (carried * key_ref[0, rows(n), :].astype(F32)).astype(BF16)
-        after = grad
+
+    before = spectrum(fwd, before_ref[...])
+    earlier = None
+    for n in range(blocks):
+        gated = spectrum(fwd, gated_ref[rows(n), :])
+        grad = spectrum(fwd, mix_ref[rows(n), :])
+        wr, wi = beside(gated, before)
+        mixed = inverse_of(inv, wr * real - wi * cross, wr * cross + wi * last)
+        out_query_ref[0, rows(n), :] = (grad_ref[0, rows(n), :].astype(F32) * mixed).astype(BF16)
+        if earlier is not None:
+            backward(n - 1, earlier, grad)
+        before, earlier = gated, grad
+    backward(blocks - 1, earlier, spectrum(fwd, after_ref[...]))
 
 
 def params():
@@ -154,13 +165,12 @@
 def shards(query_act, key_act, value_act, filter_taps, grad_out, count_all=1):
     _, row_count, chan_count = query_act.shape
     blocks = row_count // BLOCK
-    steps = chan_count // WIDTH
     fwd_np, inv_np = transform_matrices()
     fwd, inv = jnp.asarray(fwd_np), jnp.asarray(inv_np)
 
-    whole = pl.BlockSpec((1, row_count, WIDTH), lambda i: (0, 0, i))
-    stack = pl.BlockSpec((row_count, WIDTH), lambda i: (0, i))
-    slab = pl.BlockSpec((BLOCK, WIDTH), lambda i: (0, i))
+    whole = pl.BlockSpec((1, row_count, chan_count), lambda i: (0, 0, 0))
+    stack = pl.BlockSpec((row_count, chan_count), lambda i: (0, 0))
+    slab = pl.BlockSpec((BLOCK, chan_count), lambda i: (0, 0))
     fwd_spec = pl.BlockSpec(fwd.shape, lambda i: (0, 0))
     inv_spec = pl.BlockSpec(inv.shape, lambda i: (0, 0))
 
@@ -171,14 +181,26 @@
     ring = 1
     for name in ctx:
         ring *= lax.axis_size(name)
-    before = lax.ppermute(gated[row_count - BLOCK :], ctx, [(i, i + 1) for i in range(ring - 1)])
-    after = lax.ppermute(mix[:BLOCK], ctx, [(i + 1, i) for i in range(ring - 1)])
-
+    gated_edge, mix_edge = gated[row_count - BLOCK :], mix[:BLOCK]
+    first_core = lax.axis_index("c") == 0
+    inside = [(i, i + 1) for i in range(0, ring - 1, 2)]
+    outside = [(i, i + 1) for i in range(1, ring - 1, 2)]
+    both_ways = [pairs + [(j, i) for i, j in pairs] for pairs in (inside, outside)]
+    from_inside = lax.ppermute(jnp.where(first_core, gated_edge, mix_edge), ctx, both_ways[0])
+    to_outside = jnp.where(
+        first_core,
+        product(query_act[0, :BLOCK], grad_out[0, :BLOCK]),
+        product(key_act[0, row_count - BLOCK :], value_act[0, row_count - BLOCK :]),
+    )
+    from_outside = lax.ppermute(to_outside, ctx, both_ways[1])
+    before = jnp.where(first_core, from_outside, from_inside)
+    after = jnp.where(first_core, from_inside, from_outside)
+
+    close = pl.BlockSpec(memory_space=pltpu.VMEM)
     inner = pl.pallas_call(
         inner_kernel,
-        grid=(steps,),
-        in_specs=[stack, stack, fwd_spec, inv_spec],
-        out_specs=slab,
+        in_specs=[close] * 4,
+        out_specs=close,
         out_shape=jax.ShapeDtypeStruct((BLOCK, chan_count), F32),
         compiler_params=params(),
         cost_estimate=cost(800_000_000, 2_500_000),
@@ -187,14 +209,13 @@
 
     partial = pl.pallas_call(
         outer_kernel,
-        grid=(steps,),
-        in_specs=[slab, slab, slab, fwd_spec, inv_spec],
-        out_specs=pl.BlockSpec((BLOCK * WIDTH // 128, 128), lambda i: (i, 0)),
+        in_specs=[close] * 5,
+        out_specs=close,
         out_shape=jax.ShapeDtypeStruct((BLOCK * chan_count // 128, 128), BF16),
         compiler_params=params(),
         cost_estimate=cost(200_000_000, 800_000),
         name="outer_pairs",
-    )(before, mix, inner, fwd, inv)
+    )(before, mix_edge, inner, fwd, inv)
 
     near = ("xh", "c", "y", "xl")
     near_count = 1
@@ -207,7 +228,7 @@
     out_shape = jax.ShapeDtypeStruct(query_act.shape, BF16)
     grad_query, grad_key, grad_value = pl.pallas_call(
         conv_kernel,
-        grid=(steps,),
+        grid=(1,),
         in_specs=[stack, stack, whole, whole, whole, slab, slab, slab, fwd_spec, inv_spec],
         out_specs=[whole, whole, whole],
         out_shape=[out_shape, out_shape, out_shape],

time: 59.4 us -> 58.1 us (0.978)
  starting transfers between devices: 15.9 us -> 14.1 us
  Pallas kernels: 7.76 us -> 6.26 us
  other arithmetic: 2.33 us -> 3.68 us
  local copies, waits for them, and re-layouts: 0.1 us -> 0.91 us
  blocking collectives: 28.7 us -> 28.1 us
    ppermute x2, starting transfers between devices: 8.09 us -> 6.13 us  [the longest x1 6.04 us: shards(): from_outside = lax.ppermute(to_outside, ctx, both_ways[1])]
    pallas_call x3, Pallas kernels: 7.76 us -> 6.26 us  [the longest x1 3.75 us: shards(): pl.pallas_call(conv_kernel, grid=(1,), in_specs=[stack, stack, whole, who...]
    select_n x0 -> x3, other arithmetic: none -> 1.26 us  [the longest x1 1.22 us: shards(): jnp.where(first_core, product(query_act[0, :BLOCK], grad_out[0, :BLOCK]),...]
    unnamed x14 -> x12, local copies, waits for them, and re-layouts: 0.04 us -> 0.86 us
    convert_element_type x2 -> x1, other arithmetic: 1.56 us -> 1.65 us  [product(): return (left.astype(F32) * right.astype(F32)).astype(BF16)]
  transfers between devices with their start and end apart: 3 -> 3, of which waited for: 1 -> 1; matrix products, arithmetic and copies ran while one was open for 0% -> 3% of each run, Pallas kernels for 13% -> 9%
where the time goes in v3:
time: 58.1 us; the launch traced here: 57.8 us
  blocking collectives  28.1 us (48%)
  starting transfers between devices  14.1 us (24%)
  Pallas kernels  6.26 us (11%)
  waiting for transfers between devices  3.94 us (7%)
  other arithmetic  3.68 us (6%)
  local copies, waits for them, and re-layouts  0.91 us (2%)
  between operations  0.82 us (1%)
    all_to_all x1, blocking collectives, shards(): lax.all_to_all(planes, far, 0, 0, tiled=True).sum(axis=0)  15.2 us
    all_to_all x1, blocking collectives, shards(): total = lax.all_to_all(copies, near, 0, 0, tiled=True)  12.8 us
    all_to_all x1, starting transfers between devices, shards(): lax.all_to_all(chunks, near, 0, 0, tiled=True).astype(F32).sum(axis=0)  7.99 us
    ppermute x1, starting transfers between devices, shards(): from_outside = lax.ppermute(to_outside, ctx, both_ways[1])  6.04 us
    all_to_all x1, waiting for transfers between devices, shards(): lax.all_to_all(chunks, near, 0, 0, tiled=True).astype(F32).sum(axis=0)  3.94 us
    pallas_call x1, Pallas kernels, shards(): pl.pallas_call(conv_kernel, grid=(1,), in_specs=[stack, stack, whole, who...  3.75 us
    convert_element_type x1, other arithmetic, product(): return (left.astype(F32) * right.astype(F32)).astype(BF16)  1.65 us
    pallas_call x1, Pallas kernels, shards(): pl.pallas_call(outer_kernel, in_specs=[close] * 5, out_specs=close, out_s...  1.31 us
  transfers between devices with their start and end apart: 3, of which 1 were waited for; matrix products, arithmetic and copies ran while one was open for 3% of the time, Pallas kernels for 9%

profile of v3, /device:TPU:1, one launch (start us, length us, event | category | flops | bytes accessed | tf_op | source)
XLA Modules:
  0.0 57.8 jit_solution(4809339956802298002)
XLA Ops:
  0.6 0.0 copy-start
  0.6 1.2 %fusion.1 = bf16[128,512]{1,0:T(8,128)(2,1)S(1)} fusion(bf16[1,512,512]{2,1,0:T(8,128)(2,1)} %value_ref.1, bf16[1,512,512]{2,1,0:T(8,128)(2,1)} %key_ref.1, bf16[1,512,512]{2,1,0:T(8,128)(2,1)} %grad_ref.1, bf16[1,512,512]{2,1,0:T(8,128)(2,1)} %param.7, pred[]{:T(512)S(6)} %eq.3), kind=kLoop, calls=%fused_computation.7 | loop fusion | flops 589824 | bytes 655361 | tf_op jit(solution)/shard_map/jit(_where)/select_n | solution.py:190
  1.9 6.0 %collective-permute-start = (bf16[128,512]{1,0:T(8,128)(2,1)S(1)}, bf16[128,512]{1,0:T(8,128)(2,1)S(1)}, u32[]{:S(2)}, u32[]{:S(2)}) collective-permute-start(bf16[128,512]{1,0:T(8,128)(2,1)S(1)} %fusion.1), channel_id=1, source_target_pairs={{8,16},{24,32},{40,48},{56,64},{72,80},{88,96},{104,112},{120,128}... | collective-permute-start | bytes 393224 | tf_op jit(solution)/shard_map/ppermute | solution.py:195
  7.9 1.6 %multiply_convert_fusion = (bf16[1,512,512]{2,1,0:T(8,128)(2,1)S(1)}, bf16[1,512,512]{2,1,0:T(8,128)(2,1)S(1)}) fusion(bf16[1,512,512]{2,1,0:T(8,128)(2,1)S(1)} %copy-done, bf16[1,512,512]{2,1,0:T(8,128)(2,1)} %param.7, bf16[1,512,512]{2,1,0:T(8,128)(2,1)} %value_ref.1, bf16[1,512,512]{2,1,0:T(8,128)(2,1)} %key_ref.1), kind=kLoop, calls=%fused_computation | loop fusion | flops 2097152 | bytes 3145728 | tf_op jit(solution)/shard_map/convert_element_type | solution.py:72
  9.6 0.0 copy-start.3
  9.6 0.0 copy-start.4
  9.6 0.1 collective-permute-start.1
  9.7 0.8 %copy-done.3 = bf16[256,256]{1,0:T(8,128)(2,1)S(1)} copy-done((bf16[256,256]{1,0:T(8,128)(2,1)S(1)}, bf16[256,256]{1,0:T(8,128)(2,1)}, u32[]{:S(2)}) %copy-start.3) | copy-done | bytes 131096
  10.5 0.1 copy-done.4
  10.6 1.2 %inner_pairs.1.inner_ref = f32[128,512]{1,0:T(8,128)S(1)} custom-call(bf16[512,512]{1,0:T(8,128)(2,1)S(1)} %bitcast.19, bf16[512,512]{1,0:T(8,128)(2,1)S(1)} %bitcast.17, bf16[256,256]{1,0:T(8,128)(2,1)S(1)} %copy-done.4, bf16[256,256]{1,0:T(8,128)(2,1)S(1)} %copy-done.3), custom_call_target="tpu_custom_call" | custom-call | flops 800000000 | bytes 2500000 | tf_op jit(solution)/shard_map/inner_pairs/pallas_call | solution.py:200
  11.8 0.0 collective-permute-done
  11.8 0.0 collective-permute-done.1
  11.8 0.0 copy-start.1
  11.8 0.0 copy-start.2
  11.9 1.3 %outer_pairs.1 = bf16[512,128]{1,0:T(8,128)(2,1)} custom-call(bf16[128,512]{1,0:T(8,128)(2,1)S(1)} %get-tuple-element.19.halo_ref.before_ref, bf16[128,512]{1,0:T(8,128)(2,1)S(1)} %slice_bitcast_fusion.mix_ref, f32[128,512]{1,0:T(8,128)S(1)} %inner_pairs.1.inner_ref, bf16[256,256]{1,0:T(8,128)(2,1)S(1)} %copy-done.4, bf16[256,256]{1,0:T(8,128)(2,1)S(1)} %copy-done.3), custom_call_target="tpu_custom_call" | custom-call | flops 200000000 | bytes 800000 | tf_op jit(solution)/shard_map/outer_pairs/pallas_call | solution.py:210
  13.2 8.0 %all-to-all-start = ((bf16[32,16,128]{2,1,0:T(8,128)(2,1)}), bf16[32,16,128]{2,1,0:T(8,128)(2,1)S(1)}, u32[]{:S(2)}, u32[]{:S(2)}) async-start(bf16[32,16,128]{2,1,0:T(8,128)(2,1)} %bitcast.5), calls=%async_computation | async-start | bytes 262144 | tf_op jit(solution)/shard_map/all_to_all | solution.py:227
  21.2 0.0 copy-done.1
  21.2 0.0 copy-done.2
  21.2 0.0 copy-done.5
  21.2 3.8 %convolutions.1 = (bf16[1,512,512]{2,1,0:T(8,128)(2,1)}, bf16[1,512,512]{2,1,0:T(8,128)(2,1)}, bf16[1,512,512]{2,1,0:T(8,128)(2,1)}) custom-call(bf16[512,512]{1,0:T(8,128)(2,1)S(1)} %bitcast.20, bf16[512,512]{1,0:T(8,128)(2,1)S(1)} %bitcast.18, bf16[1,512,512]{2,1,0:T(8,128)(2,1)S(1)} %copy-done.2, bf16[1,512,512]{2,1,0:T(8,128)(2,1)S(1)} %copy-done.1, ...), custom_call_target="tpu_custom_call" | custom-call | flops 2000000000 | bytes 4000000 | tf_op jit(solution)/shard_map/convolutions/pallas_call | solution.py:229
  24.9 3.9 %all-to-all-done = bf16[32,16,128]{2,1,0:T(8,128)(2,1)S(1)} async-done(((bf16[32,16,128]{2,1,0:T(8,128)(2,1)}), bf16[32,16,128]{2,1,0:T(8,128)(2,1)S(1)}, u32[]{:S(2)}, u32[]{:S(2)}) %all-to-all-start) | async-done | bytes 131104 | tf_op jit(solution)/shard_map/all_to_all | solution.py:227
  28.9 15.2 %all_to_all.15 = f32[8,16,128]{2,1,0:T(8,128)S(1)} all-to-all(f32[8,16,128]{2,1,0:T(8,128)S(1)} %broadcast_in_dim.4), channel_id=1, replica_groups=mesh['z'=8,'xh'=2,'c'=2,'y'=4,'xl'=2] {'z'}, dimensions={0} | all-to-all | bytes 131072 | tf_op jit(solution)/shard_map/all_to_all | solution.py:243
  44.2 12.8 %all_to_all.16 = bf16[32,16,128]{2,1,0:T(8,128)(2,1)S(1)} all-to-all(bf16[32,16,128]{2,1,0:T(8,128)(2,1)S(1)} %broadcast_in_dim.5), channel_id=1, replica_groups=mesh['z'=8,'xh'=2,'c'=2,'y'=4,'xl'=2] {'xh','c','y','xl'}, dimensions={0} | all-to-all | bytes 262144 | tf_op jit(solution)/shard_map/all_to_all | solution.py:245
  57.1 0.7 %pad_maximum_fusion = f32[128,512]{1,0:T(8,128)} fusion(f32[128,128]{1,0:T(8,128)S(1)} %bitcast.24, f32[128,128]{1,0:T(8,128)S(1)} %bitcast.23, f32[128,128]{1,0:T(8,128)S(1)} %bitcast.22, f32[128,128]{1,0:T(8,128)S(1)} %bitcast.21), kind=kLoop, calls=%fused_computation.2 | loop fusion | flops 196608 | bytes 524288 | tf_op jit(solution)/shard_map/concatenate | solution.py:247
  (11 shorter events, 0.2 us)
Async XLA Ops:
  0.6 7.3 %copy-start = (bf16[1,512,512]{2,1,0:T(8,128)(2,1)S(1)}, bf16[1,512,512]{2,1,0:T(8,128)(2,1)}, u32[]{:S(2)}) copy-start(bf16[1,512,512]{2,1,0:T(8,128)(2,1)} %grad_ref.1) | copy-start | bytes 1572868
  1.9 9.9 %collective-permute-start = (bf16[128,512]{1,0:T(8,128)(2,1)S(1)}, bf16[128,512]{1,0:T(8,128)(2,1)S(1)}, u32[]{:S(2)}, u32[]{:S(2)}) collective-permute-start(bf16[128,512]{1,0:T(8,128)(2,1)S(1)} %fusion.1), channel_id=1, source_target_pairs={{8,16},{24,32},{40,48},{56,64},{72,80},{88,96},{104,112},{120,128}... | collective-permute-start | bytes 393224 | tf_op jit(solution)/shard_map/ppermute | solution.py:195
  9.6 0.9 %copy-start.3 = (bf16[256,256]{1,0:T(8,128)(2,1)S(1)}, bf16[256,256]{1,0:T(8,128)(2,1)}, u32[]{:S(2)}) copy-start(bf16[256,256]{1,0:T(8,128)(2,1)} %constant.18.clone.inv_ref) | copy-start | bytes 393220
  9.6 1.0 %copy-start.4 = (bf16[256,256]{1,0:T(8,128)(2,1)S(1)}, bf16[256,256]{1,0:T(8,128)(2,1)}, u32[]{:S(2)}) copy-start(bf16[256,256]{1,0:T(8,128)(2,1)} %constant.17.clone.fwd_ref) | copy-start | bytes 393220
  9.6 2.2 %collective-permute-start.1 = (bf16[128,512]{1,0:T(8,128)(2,1)S(1)}, bf16[128,512]{1,0:T(8,128)(2,1)S(1)}, u32[]{:S(2)}, u32[]{:S(2)}) collective-permute-start(bf16[128,512]{1,0:T(8,128)(2,1)S(1)} %fusion.2), channel_id=1, source_target_pairs={{0,8},{16,24},{32,40},{48,56},{64,72},{80,88},{96,104},{112,120},{... | collective-permute-start | bytes 393224 | tf_op jit(solution)/shard_map/ppermute | solution.py:189
  11.8 9.3 %copy-start.1 = (bf16[1,512,512]{2,1,0:T(8,128)(2,1)S(1)}, bf16[1,512,512]{2,1,0:T(8,128)(2,1)}, u32[]{:S(2)}) copy-start(bf16[1,512,512]{2,1,0:T(8,128)(2,1)} %value_ref.1) | copy-start | bytes 1572868
  11.8 9.3 %copy-start.2 = (bf16[1,512,512]{2,1,0:T(8,128)(2,1)S(1)}, bf16[1,512,512]{2,1,0:T(8,128)(2,1)}, u32[]{:S(2)}) copy-start(bf16[1,512,512]{2,1,0:T(8,128)(2,1)} %key_ref.1) | copy-start | bytes 1572868
  13.2 8.0 %copy-start.5 = (bf16[128,512]{1,0:T(8,128)(2,1)S(1)}, bf16[128,512]{1,0:T(8,128)(2,1)}, u32[]{:S(2)}) copy-start(bf16[128,512]{1,0:T(8,128)(2,1)} %taps_ref.1) | copy-start | bytes 393220
  13.2 15.7 %all-to-all-start = ((bf16[32,16,128]{2,1,0:T(8,128)(2,1)}), bf16[32,16,128]{2,1,0:T(8,128)(2,1)S(1)}, u32[]{:S(2)}, u32[]{:S(2)}) async-start(bf16[32,16,128]{2,1,0:T(8,128)(2,1)} %bitcast.5), calls=%async_computation | async-start | bytes 262144 | tf_op jit(solution)/shard_map/all_to_all | solution.py:227

commit v4 on v3

--- a/solution.py
+++ b/solution.py
@@ -217,7 +217,7 @@
         name="outer_pairs",
     )(before, mix_edge, inner, fwd, inv)
 
-    near = ("xh", "c", "y", "xl")
+    near = ("c", "xh", "xl", "y")
     near_count = 1
     for name in near:
         near_count *= lax.axis_size(name)
@@ -239,8 +239,8 @@
     mine, grad_query, grad_key, grad_value = lax.optimization_barrier(
         (mine, grad_query, grad_key, grad_value)
     )
-    planes = jnp.broadcast_to(mine[None], (far_count,) + mine.shape)
-    mine = lax.all_to_all(planes, far, 0, 0, tiled=True).sum(axis=0) / math.sqrt(count_all)
+    planes = jnp.broadcast_to(mine.astype(BF16)[None], (far_count,) + mine.shape)
+    mine = lax.all_to_all(planes, far, 0, 0, tiled=True).astype(F32).sum(axis=0) / math.sqrt(count_all)
     copies = jnp.broadcast_to(mine.astype(BF16)[None], (near_count,) + mine.shape)
     total = lax.all_to_all(copies, near, 0, 0, tiled=True)
     total = total.reshape(chan_count // 128, BLOCK, 128).astype(F32)

time: 58.1 us -> 57.4 us (0.988)
  no operation moved by 1% of the time
where the time goes in v4:
time: 57.4 us; the launch traced here: 57.1 us
  blocking collectives  27.6 us (48%)
  starting transfers between devices  14.1 us (25%)
  Pallas kernels  6.26 us (11%)
  waiting for transfers between devices  3.75 us (7%)
  other arithmetic  3.68 us (6%)
  local copies, waits for them, and re-layouts  0.91 us (2%)
  between operations  0.82 us (1%)
    all_to_all x1, blocking collectives, shards(): lax.all_to_all(planes, far, 0, 0, tiled=True).astype(F32).sum(axis=0)  14.9 us
    all_to_all x1, blocking collectives, shards(): total = lax.all_to_all(copies, near, 0, 0, tiled=True)  12.7 us
    all_to_all x1, starting transfers between devices, shards(): lax.all_to_all(chunks, near, 0, 0, tiled=True).astype(F32).sum(axis=0)  7.99 us
    ppermute x1, starting transfers between devices, shards(): from_outside = lax.ppermute(to_outside, ctx, both_ways[1])  6.04 us
    pallas_call x1, Pallas kernels, shards(): pl.pallas_call(conv_kernel, grid=(1,), in_specs=[stack, stack, whole, who...  3.76 us
    all_to_all x1, waiting for transfers between devices, shards(): lax.all_to_all(chunks, near, 0, 0, tiled=True).astype(F32).sum(axis=0)  3.75 us
    convert_element_type x1, other arithmetic, product(): return (left.astype(F32) * right.astype(F32)).astype(BF16)  1.65 us
    pallas_call x1, Pallas kernels, shards(): pl.pallas_call(outer_kernel, in_specs=[close] * 5, out_specs=close, out_s...  1.31 us
  transfers between devices with their start and end apart: 3, of which 1 were waited for; matrix products, arithmetic and copies ran while one was open for 3% of the time, Pallas kernels for 9%

profile of v4, /device:TPU:1, one launch (start us, length us, event | category | flops | bytes accessed | tf_op | source)
XLA Modules:
  0.0 57.1 jit_solution(13269903879099453893)
XLA Ops:
  0.6 0.0 copy-start
  0.6 1.2 %fusion.1 = bf16[128,512]{1,0:T(8,128)(2,1)S(1)} fusion(bf16[1,512,512]{2,1,0:T(8,128)(2,1)} %value_ref.1, bf16[1,512,512]{2,1,0:T(8,128)(2,1)} %key_ref.1, bf16[1,512,512]{2,1,0:T(8,128)(2,1)} %grad_ref.1, bf16[1,512,512]{2,1,0:T(8,128)(2,1)} %param.7, pred[]{:T(512)S(6)} %eq.3), kind=kLoop, calls=%fused_computation.7 | loop fusion | flops 589824 | bytes 655361 | tf_op jit(solution)/shard_map/jit(_where)/select_n | solution.py:190
  1.9 6.0 %collective-permute-start = (bf16[128,512]{1,0:T(8,128)(2,1)S(1)}, bf16[128,512]{1,0:T(8,128)(2,1)S(1)}, u32[]{:S(2)}, u32[]{:S(2)}) collective-permute-start(bf16[128,512]{1,0:T(8,128)(2,1)S(1)} %fusion.1), channel_id=1, source_target_pairs={{8,16},{24,32},{40,48},{56,64},{72,80},{88,96},{104,112},{120,128}... | collective-permute-start | bytes 393224 | tf_op jit(solution)/shard_map/ppermute | solution.py:195
  7.9 0.0 copy-done
  7.9 1.6 %multiply_convert_fusion = (bf16[1,512,512]{2,1,0:T(8,128)(2,1)S(1)}, bf16[1,512,512]{2,1,0:T(8,128)(2,1)S(1)}) fusion(bf16[1,512,512]{2,1,0:T(8,128)(2,1)S(1)} %copy-done, bf16[1,512,512]{2,1,0:T(8,128)(2,1)} %param.7, bf16[1,512,512]{2,1,0:T(8,128)(2,1)} %value_ref.1, bf16[1,512,512]{2,1,0:T(8,128)(2,1)} %key_ref.1), kind=kLoop, calls=%fused_computation | loop fusion | flops 2097152 | bytes 3145728 | tf_op jit(solution)/shard_map/convert_element_type | solution.py:72
  9.6 0.0 copy-start.3
  9.6 0.0 copy-start.4
  9.6 0.1 collective-permute-start.1
  9.7 0.8 %copy-done.3 = bf16[256,256]{1,0:T(8,128)(2,1)S(1)} copy-done((bf16[256,256]{1,0:T(8,128)(2,1)S(1)}, bf16[256,256]{1,0:T(8,128)(2,1)}, u32[]{:S(2)}) %copy-start.3) | copy-done | bytes 131096
  10.5 0.1 copy-done.4
  10.6 1.2 %inner_pairs.1.inner_ref = f32[128,512]{1,0:T(8,128)S(1)} custom-call(bf16[512,512]{1,0:T(8,128)(2,1)S(1)} %bitcast.19, bf16[512,512]{1,0:T(8,128)(2,1)S(1)} %bitcast.17, bf16[256,256]{1,0:T(8,128)(2,1)S(1)} %copy-done.4, bf16[256,256]{1,0:T(8,128)(2,1)S(1)} %copy-done.3), custom_call_target="tpu_custom_call" | custom-call | flops 800000000 | bytes 2500000 | tf_op jit(solution)/shard_map/inner_pairs/pallas_call | solution.py:200
  11.8 0.0 collective-permute-done
  11.8 0.0 collective-permute-done.1
  11.8 0.0 copy-start.1
  11.8 0.0 copy-start.2
  11.9 1.3 %outer_pairs.1 = bf16[512,128]{1,0:T(8,128)(2,1)} custom-call(bf16[128,512]{1,0:T(8,128)(2,1)S(1)} %get-tuple-element.19.halo_ref.before_ref, bf16[128,512]{1,0:T(8,128)(2,1)S(1)} %slice_bitcast_fusion.mix_ref, f32[128,512]{1,0:T(8,128)S(1)} %inner_pairs.1.inner_ref, bf16[256,256]{1,0:T(8,128)(2,1)S(1)} %copy-done.4, bf16[256,256]{1,0:T(8,128)(2,1)S(1)} %copy-done.3), custom_call_target="tpu_custom_call" | custom-call | flops 200000000 | bytes 800000 | tf_op jit(solution)/shard_map/outer_pairs/pallas_call | solution.py:210
  13.2 8.0 %all-to-all-start = ((bf16[32,16,128]{2,1,0:T(8,128)(2,1)}), bf16[32,16,128]{2,1,0:T(8,128)(2,1)S(1)}, u32[]{:S(2)}, u32[]{:S(2)}) async-start(bf16[32,16,128]{2,1,0:T(8,128)(2,1)} %bitcast.5), calls=%async_computation | async-start | bytes 262144 | tf_op jit(solution)/shard_map/all_to_all | solution.py:227
  21.2 0.0 copy-done.1
  21.2 0.0 copy-done.2
  21.2 3.8 %convolutions.1 = (bf16[1,512,512]{2,1,0:T(8,128)(2,1)}, bf16[1,512,512]{2,1,0:T(8,128)(2,1)}, bf16[1,512,512]{2,1,0:T(8,128)(2,1)}) custom-call(bf16[512,512]{1,0:T(8,128)(2,1)S(1)} %bitcast.20, bf16[512,512]{1,0:T(8,128)(2,1)S(1)} %bitcast.18, bf16[1,512,512]{2,1,0:T(8,128)(2,1)S(1)} %copy-done.2, bf16[1,512,512]{2,1,0:T(8,128)(2,1)S(1)} %copy-done.1, ...), custom_call_target="tpu_custom_call" | custom-call | flops 2000000000 | bytes 4000000 | tf_op jit(solution)/shard_map/convolutions/pallas_call | solution.py:229
  25.0 3.7 %all-to-all-done = bf16[32,16,128]{2,1,0:T(8,128)(2,1)S(1)} async-done(((bf16[32,16,128]{2,1,0:T(8,128)(2,1)}), bf16[32,16,128]{2,1,0:T(8,128)(2,1)S(1)}, u32[]{:S(2)}, u32[]{:S(2)}) %all-to-all-start) | async-done | bytes 131104 | tf_op jit(solution)/shard_map/all_to_all | solution.py:227
  28.8 14.9 %all_to_all.15 = bf16[8,16,128]{2,1,0:T(8,128)(2,1)S(1)} all-to-all(bf16[8,16,128]{2,1,0:T(8,128)(2,1)S(1)} %broadcast_in_dim.4), channel_id=1, replica_groups=mesh['z'=8,'xh'=2,'c'=2,'y'=4,'xl'=2] {'z'}, dimensions={0} | all-to-all | bytes 65536 | tf_op jit(solution)/shard_map/all_to_all | solution.py:243
  43.7 12.7 %all_to_all.16 = bf16[32,16,128]{2,1,0:T(8,128)(2,1)S(1)} all-to-all(bf16[32,16,128]{2,1,0:T(8,128)(2,1)S(1)} %broadcast_in_dim.5), channel_id=1, replica_groups=mesh['z'=8,'xh'=2,'c'=2,'y'=4,'xl'=2] {'c','xh','xl','y'}, dimensions={0} | all-to-all | bytes 262144 | tf_op jit(solution)/shard_map/all_to_all | solution.py:245
  56.4 0.7 %pad_maximum_fusion = f32[128,512]{1,0:T(8,128)} fusion(f32[128,128]{1,0:T(8,128)S(1)} %bitcast.24, f32[128,128]{1,0:T(8,128)S(1)} %bitcast.23, f32[128,128]{1,0:T(8,128)S(1)} %bitcast.22, f32[128,128]{1,0:T(8,128)S(1)} %bitcast.21), kind=kLoop, calls=%fused_computation.2 | loop fusion | flops 196608 | bytes 524288 | tf_op jit(solution)/shard_map/concatenate | solution.py:247
  (11 shorter events, 0.2 us)
Async XLA Ops:
  0.6 7.3 %copy-start = (bf16[1,512,512]{2,1,0:T(8,128)(2,1)S(1)}, bf16[1,512,512]{2,1,0:T(8,128)(2,1)}, u32[]{:S(2)}) copy-start(bf16[1,512,512]{2,1,0:T(8,128)(2,1)} %grad_ref.1) | copy-start | bytes 1572868
  1.9 9.9 %collective-permute-start = (bf16[128,512]{1,0:T(8,128)(2,1)S(1)}, bf16[128,512]{1,0:T(8,128)(2,1)S(1)}, u32[]{:S(2)}, u32[]{:S(2)}) collective-permute-start(bf16[128,512]{1,0:T(8,128)(2,1)S(1)} %fusion.1), channel_id=1, source_target_pairs={{8,16},{24,32},{40,48},{56,64},{72,80},{88,96},{104,112},{120,128}... | collective-permute-start | bytes 393224 | tf_op jit(solution)/shard_map/ppermute | solution.py:195
  9.6 0.9 %copy-start.3 = (bf16[256,256]{1,0:T(8,128)(2,1)S(1)}, bf16[256,256]{1,0:T(8,128)(2,1)}, u32[]{:S(2)}) copy-start(bf16[256,256]{1,0:T(8,128)(2,1)} %constant.18.clone.inv_ref) | copy-start | bytes 393220
  9.6 1.0 %copy-start.4 = (bf16[256,256]{1,0:T(8,128)(2,1)S(1)}, bf16[256,256]{1,0:T(8,128)(2,1)}, u32[]{:S(2)}) copy-start(bf16[256,256]{1,0:T(8,128)(2,1)} %constant.17.clone.fwd_ref) | copy-start | bytes 393220
  9.6 2.2 %collective-permute-start.1 = (bf16[128,512]{1,0:T(8,128)(2,1)S(1)}, bf16[128,512]{1,0:T(8,128)(2,1)S(1)}, u32[]{:S(2)}, u32[]{:S(2)}) collective-permute-start(bf16[128,512]{1,0:T(8,128)(2,1)S(1)} %fusion.2), channel_id=1, source_target_pairs={{0,8},{16,24},{32,40},{48,56},{64,72},{80,88},{96,104},{112,120},{... | collective-permute-start | bytes 393224 | tf_op jit(solution)/shard_map/ppermute | solution.py:189
  11.8 9.3 %copy-start.1 = (bf16[1,512,512]{2,1,0:T(8,128)(2,1)S(1)}, bf16[1,512,512]{2,1,0:T(8,128)(2,1)}, u32[]{:S(2)}) copy-start(bf16[1,512,512]{2,1,0:T(8,128)(2,1)} %value_ref.1) | copy-start | bytes 1572868
  11.8 9.3 %copy-start.2 = (bf16[1,512,512]{2,1,0:T(8,128)(2,1)S(1)}, bf16[1,512,512]{2,1,0:T(8,128)(2,1)}, u32[]{:S(2)}) copy-start(bf16[1,512,512]{2,1,0:T(8,128)(2,1)} %key_ref.1) | copy-start | bytes 1572868
  13.2 8.0 %copy-start.5 = (bf16[128,512]{1,0:T(8,128)(2,1)S(1)}, bf16[128,512]{1,0:T(8,128)(2,1)}, u32[]{:S(2)}) copy-start(bf16[128,512]{1,0:T(8,128)(2,1)} %taps_ref.1) | copy-start | bytes 393220
  13.2 15.5 %all-to-all-start = ((bf16[32,16,128]{2,1,0:T(8,128)(2,1)}), bf16[32,16,128]{2,1,0:T(8,128)(2,1)S(1)}, u32[]{:S(2)}, u32[]{:S(2)}) async-start(bf16[32,16,128]{2,1,0:T(8,128)(2,1)} %bitcast.5), calls=%async_computation | async-start | bytes 262144 | tf_op jit(solution)/shard_map/all_to_all | solution.py:227

commit v5 on v4

--- a/solution.py
+++ b/solution.py
@@ -225,6 +225,7 @@
     far_count = lax.axis_size(far)
     chunks = partial.reshape(near_count, -1, 128)
     mine = lax.all_to_all(chunks, near, 0, 0, tiled=True).astype(F32).sum(axis=0)
+    mine, before, after = lax.optimization_barrier((mine, before, after))
     out_shape = jax.ShapeDtypeStruct(query_act.shape, BF16)
     grad_query, grad_key, grad_value = pl.pallas_call(
         conv_kernel,
@@ -236,11 +237,11 @@
         cost_estimate=cost(2_000_000_000, 4_000_000),
         name="convolutions",
     )(gated, mix, key_act, value_act, grad_out, before, after, filter_taps, fwd, inv)
+    planes = jnp.broadcast_to(mine.astype(BF16)[None], (far_count,) + mine.shape)
+    mine = lax.all_to_all(planes, far, 0, 0, tiled=True).astype(F32).sum(axis=0) / math.sqrt(count_all)
     mine, grad_query, grad_key, grad_value = lax.optimization_barrier(
         (mine, grad_query, grad_key, grad_value)
     )
-    planes = jnp.broadcast_to(mine.astype(BF16)[None], (far_count,) + mine.shape)
-    mine = lax.all_to_all(planes, far, 0, 0, tiled=True).astype(F32).sum(axis=0) / math.sqrt(count_all)
     copies = jnp.broadcast_to(mine.astype(BF16)[None], (near_count,) + mine.shape)
     total = lax.all_to_all(copies, near, 0, 0, tiled=True)
     total = total.reshape(chan_count // 128, BLOCK, 128).astype(F32)

time: 57.4 us -> 57.2 us (level)
  Pallas kernels: 6.26 us -> 5.6 us
  waiting for transfers between devices: 3.75 us -> 3.11 us
  local copies, waits for them, and re-layouts: 0.91 us -> 1.53 us
    pallas_call x1, Pallas kernels: 1.31 us -> 0.65 us  [shards(): pl.pallas_call(outer_kernel, in_specs=[close] * 5, out_specs=close, out_s...]
    all_to_all x1, waiting for transfers between devices: 3.75 us -> 3.1 us  [shards(): lax.all_to_all(planes, far, 0, 0, tiled=True).astype(F32).sum(axis=0)]
    broadcast_in_dim x1, local copies, waits for them, and re-layouts: 0.01 us -> 0.62 us  [shards(): jnp.broadcast_to(mine.astype(BF16)[None], (far_count,) + mine.shape)]
where the time goes in v5:
time: 57.2 us; the launch traced here: 56.9 us
  blocking collectives  27.9 us (49%)
  starting transfers between devices  14.3 us (25%)
  Pallas kernels  5.6 us (10%)
  other arithmetic  3.68 us (6%)
  waiting for transfers between devices  3.11 us (5%)
  local copies, waits for them, and re-layouts  1.53 us (3%)
  between operations  0.81 us (1%)
    all_to_all x1, blocking collectives, shards(): lax.all_to_all(chunks, near, 0, 0, tiled=True).astype(F32).sum(axis=0)  15.2 us
    all_to_all x1, blocking collectives, shards(): total = lax.all_to_all(copies, near, 0, 0, tiled=True)  12.7 us
    all_to_all x1, starting transfers between devices, shards(): lax.all_to_all(planes, far, 0, 0, tiled=True).astype(F32).sum(axis=0)  8.19 us
    ppermute x1, starting transfers between devices, shards(): from_outside = lax.ppermute(to_outside, ctx, both_ways[1])  6.04 us
    pallas_call x1, Pallas kernels, shards(): pl.pallas_call(conv_kernel, grid=(1,), in_specs=[stack, stack, whole, who...  3.75 us
    all_to_all x1, waiting for transfers between devices, shards(): lax.all_to_all(planes, far, 0, 0, tiled=True).astype(F32).sum(axis=0)  3.1 us
    convert_element_type x1, other arithmetic, product(): return (left.astype(F32) * right.astype(F32)).astype(BF16)  1.65 us
    select_n x1, other arithmetic, shards(): jnp.where(first_core, product(query_act[0, :BLOCK], grad_out[0, :BLOCK]),...  1.22 us
  transfers between devices with their start and end apart: 3, of which 1 were waited for; matrix products, arithmetic and copies ran while one was open for 3% of the time, Pallas kernels for 9%

profile of v5, /device:TPU:1, one launch (start us, length us, event | category | flops | bytes accessed | tf_op | source)
XLA Modules:
  0.0 56.9 jit_solution(3321516877795672460)
XLA Ops:
  0.6 0.0 copy-start
  0.6 1.2 %fusion.1 = bf16[128,512]{1,0:T(8,128)(2,1)S(1)} fusion(bf16[1,512,512]{2,1,0:T(8,128)(2,1)} %value_ref.1, bf16[1,512,512]{2,1,0:T(8,128)(2,1)} %key_ref.1, bf16[1,512,512]{2,1,0:T(8,128)(2,1)} %grad_ref.1, bf16[1,512,512]{2,1,0:T(8,128)(2,1)} %param.7, pred[]{:T(512)S(6)} %eq.3), kind=kLoop, calls=%fused_computation.7 | loop fusion | flops 589824 | bytes 655361 | tf_op jit(solution)/shard_map/jit(_where)/select_n | solution.py:190
  1.9 6.0 %collective-permute-start = (bf16[128,512]{1,0:T(8,128)(2,1)S(1)}, bf16[128,512]{1,0:T(8,128)(2,1)S(1)}, u32[]{:S(2)}, u32[]{:S(2)}) collective-permute-start(bf16[128,512]{1,0:T(8,128)(2,1)S(1)} %fusion.1), channel_id=1, source_target_pairs={{8,16},{24,32},{40,48},{56,64},{72,80},{88,96},{104,112},{120,128}... | collective-permute-start | bytes 393224 | tf_op jit(solution)/shard_map/ppermute | solution.py:195
  7.9 0.0 copy-done
  7.9 1.6 %multiply_convert_fusion = (bf16[1,512,512]{2,1,0:T(8,128)(2,1)S(1)}, bf16[1,512,512]{2,1,0:T(8,128)(2,1)S(1)}) fusion(bf16[1,512,512]{2,1,0:T(8,128)(2,1)S(1)} %copy-done, bf16[1,512,512]{2,1,0:T(8,128)(2,1)} %param.7, bf16[1,512,512]{2,1,0:T(8,128)(2,1)} %value_ref.1, bf16[1,512,512]{2,1,0:T(8,128)(2,1)} %key_ref.1), kind=kLoop, calls=%fused_computation | loop fusion | flops 2097152 | bytes 3145728 | tf_op jit(solution)/shard_map/convert_element_type | solution.py:72
  9.6 0.0 copy-start.3
  9.6 0.0 copy-start.4
  9.6 0.1 collective-permute-start.1
  9.7 0.8 %copy-done.3 = bf16[256,256]{1,0:T(8,128)(2,1)S(1)} copy-done((bf16[256,256]{1,0:T(8,128)(2,1)S(1)}, bf16[256,256]{1,0:T(8,128)(2,1)}, u32[]{:S(2)}) %copy-start.3) | copy-done | bytes 131096
  10.5 0.1 copy-done.4
  10.6 1.2 %inner_pairs.1.inner_ref = f32[128,512]{1,0:T(8,128)S(1)} custom-call(bf16[512,512]{1,0:T(8,128)(2,1)S(1)} %bitcast.19, bf16[512,512]{1,0:T(8,128)(2,1)S(1)} %bitcast.17, bf16[256,256]{1,0:T(8,128)(2,1)S(1)} %copy-done.4, bf16[256,256]{1,0:T(8,128)(2,1)S(1)} %copy-done.3), custom_call_target="tpu_custom_call" | custom-call | flops 800000000 | bytes 2500000 | tf_op jit(solution)/shard_map/inner_pairs/pallas_call | solution.py:200
  11.8 0.0 collective-permute-done
  11.8 0.0 collective-permute-done.1
  11.8 0.0 copy-start.1
  11.8 0.0 copy-start.2
  11.9 0.7 %outer_pairs.1 = bf16[512,128]{1,0:T(8,128)(2,1)S(1)} custom-call(bf16[128,512]{1,0:T(8,128)(2,1)S(1)} %get-tuple-element.15.halo_ref.before_ref, bf16[128,512]{1,0:T(8,128)(2,1)S(1)} %slice_bitcast_fusion.mix_ref, f32[128,512]{1,0:T(8,128)S(1)} %inner_pairs.1.inner_ref, bf16[256,256]{1,0:T(8,128)(2,1)S(1)} %copy-done.4, bf16[256,256]{1,0:T(8,128)(2,1)S(1)} %copy-done.3), custom_call_target="tpu_custom_call" | custom-call | flops 200000000 | bytes 800000 | tf_op jit(solution)/shard_map/outer_pairs/pallas_call | solution.py:210
  12.5 15.2 %all_to_all.15 = bf16[32,16,128]{2,1,0:T(8,128)(2,1)S(1)} all-to-all(bf16[32,16,128]{2,1,0:T(8,128)(2,1)S(1)} %bitcast.21), channel_id=1, replica_groups=mesh['z'=8,'xh'=2,'c'=2,'y'=4,'xl'=2] {'c','xh','xl','y'}, dimensions={0} | all-to-all | bytes 262144 | tf_op jit(solution)/shard_map/all_to_all | solution.py:227
  27.7 0.6 %broadcast_in_dim.4 = bf16[8,16,128]{2,1,0:T(8,128)(2,1)} broadcast(bf16[16,128]{1,0:T(8,128)(2,1)S(1)} %convert_reduce_fusion), dimensions={1,2} | broadcast | bytes 36864 | tf_op jit(solution)/shard_map/broadcast_in_dim | solution.py:240
  28.4 8.2 %all-to-all-start.1 = ((bf16[8,16,128]{2,1,0:T(8,128)(2,1)}), bf16[8,16,128]{2,1,0:T(8,128)(2,1)S(1)}, u32[]{:S(2)}, u32[]{:S(2)}) async-start(bf16[8,16,128]{2,1,0:T(8,128)(2,1)} %broadcast_in_dim.4), calls=%async_computation.1 | async-start | bytes 65536 | tf_op jit(solution)/shard_map/all_to_all | solution.py:241
  36.6 0.0 copy-done.1
  36.6 3.8 %convolutions.1 = (bf16[1,512,512]{2,1,0:T(8,128)(2,1)}, bf16[1,512,512]{2,1,0:T(8,128)(2,1)}, bf16[1,512,512]{2,1,0:T(8,128)(2,1)}) custom-call(bf16[512,512]{1,0:T(8,128)(2,1)S(1)} %bitcast.20, bf16[512,512]{1,0:T(8,128)(2,1)S(1)} %bitcast.18, bf16[1,512,512]{2,1,0:T(8,128)(2,1)S(1)} %copy-done.2, bf16[1,512,512]{2,1,0:T(8,128)(2,1)S(1)} %copy-done.1, ...), custom_call_target="tpu_custom_call" | custom-call | flops 2000000000 | bytes 4000000 | tf_op jit(solution)/shard_map/convolutions/pallas_call | solution.py:230
  40.3 3.1 %all-to-all-done.1 = bf16[8,16,128]{2,1,0:T(8,128)(2,1)S(1)} async-done(((bf16[8,16,128]{2,1,0:T(8,128)(2,1)}), bf16[8,16,128]{2,1,0:T(8,128)(2,1)S(1)}, u32[]{:S(2)}, u32[]{:S(2)}) %all-to-all-start.1) | async-done | bytes 32800 | tf_op jit(solution)/shard_map/all_to_all | solution.py:241
  43.5 12.7 %all_to_all.16 = bf16[32,16,128]{2,1,0:T(8,128)(2,1)S(1)} all-to-all(bf16[32,16,128]{2,1,0:T(8,128)(2,1)S(1)} %broadcast_in_dim.5), channel_id=1, replica_groups=mesh['z'=8,'xh'=2,'c'=2,'y'=4,'xl'=2] {'c','xh','xl','y'}, dimensions={0} | all-to-all | bytes 262144 | tf_op jit(solution)/shard_map/all_to_all | solution.py:246
  56.2 0.7 %pad_maximum_fusion = f32[128,512]{1,0:T(8,128)} fusion(f32[128,128]{1,0:T(8,128)S(1)} %bitcast.25, f32[128,128]{1,0:T(8,128)S(1)} %bitcast.24, f32[128,128]{1,0:T(8,128)S(1)} %bitcast.23, f32[128,128]{1,0:T(8,128)S(1)} %bitcast.22), kind=kLoop, calls=%fused_computation.2 | loop fusion | flops 196608 | bytes 524288 | tf_op jit(solution)/shard_map/concatenate | solution.py:248
  (11 shorter events, 0.1 us)
Async XLA Ops:
  0.6 7.3 %copy-start = (bf16[1,512,512]{2,1,0:T(8,128)(2,1)S(1)}, bf16[1,512,512]{2,1,0:T(8,128)(2,1)}, u32[]{:S(2)}) copy-start(bf16[1,512,512]{2,1,0:T(8,128)(2,1)} %grad_ref.1) | copy-start | bytes 1572868
  1.9 9.9 %collective-permute-start = (bf16[128,512]{1,0:T(8,128)(2,1)S(1)}, bf16[128,512]{1,0:T(8,128)(2,1)S(1)}, u32[]{:S(2)}, u32[]{:S(2)}) collective-permute-start(bf16[128,512]{1,0:T(8,128)(2,1)S(1)} %fusion.1), channel_id=1, source_target_pairs={{8,16},{24,32},{40,48},{56,64},{72,80},{88,96},{104,112},{120,128}... | collective-permute-start | bytes 393224 | tf_op jit(solution)/shard_map/ppermute | solution.py:195
  9.6 0.9 %copy-start.3 = (bf16[256,256]{1,0:T(8,128)(2,1)S(1)}, bf16[256,256]{1,0:T(8,128)(2,1)}, u32[]{:S(2)}) copy-start(bf16[256,256]{1,0:T(8,128)(2,1)} %constant.18.clone.inv_ref) | copy-start | bytes 393220
  9.6 1.0 %copy-start.4 = (bf16[256,256]{1,0:T(8,128)(2,1)S(1)}, bf16[256,256]{1,0:T(8,128)(2,1)}, u32[]{:S(2)}) copy-start(bf16[256,256]{1,0:T(8,128)(2,1)} %constant.17.clone.fwd_ref) | copy-start | bytes 393220
  9.6 2.2 %collective-permute-start.1 = (bf16[128,512]{1,0:T(8,128)(2,1)S(1)}, bf16[128,512]{1,0:T(8,128)(2,1)S(1)}, u32[]{:S(2)}, u32[]{:S(2)}) collective-permute-start(bf16[128,512]{1,0:T(8,128)(2,1)S(1)} %fusion.2), channel_id=1, source_target_pairs={{0,8},{16,24},{32,40},{48,56},{64,72},{80,88},{96,104},{112,120},{... | collective-permute-start | bytes 393224 | tf_op jit(solution)/shard_map/ppermute | solution.py:189
  11.8 24.7 %copy-start.1 = (bf16[1,512,512]{2,1,0:T(8,128)(2,1)S(1)}, bf16[1,512,512]{2,1,0:T(8,128)(2,1)}, u32[]{:S(2)}) copy-start(bf16[1,512,512]{2,1,0:T(8,128)(2,1)} %value_ref.1) | copy-start | bytes 1572868
  11.8 24.7 %copy-start.2 = (bf16[1,512,512]{2,1,0:T(8,128)(2,1)S(1)}, bf16[1,512,512]{2,1,0:T(8,128)(2,1)}, u32[]{:S(2)}) copy-start(bf16[1,512,512]{2,1,0:T(8,128)(2,1)} %key_ref.1) | copy-start | bytes 1572868
  27.7 8.9 %copy-start.5 = (bf16[128,512]{1,0:T(8,128)(2,1)S(1)}, bf16[128,512]{1,0:T(8,128)(2,1)}, u32[]{:S(2)}) copy-start(bf16[128,512]{1,0:T(8,128)(2,1)} %taps_ref.1) | copy-start | bytes 393220
  28.4 15.1 %all-to-all-start.1 = ((bf16[8,16,128]{2,1,0:T(8,128)(2,1)}), bf16[8,16,128]{2,1,0:T(8,128)(2,1)S(1)}, u32[]{:S(2)}, u32[]{:S(2)}) async-start(bf16[8,16,128]{2,1,0:T(8,128)(2,1)} %broadcast_in_dim.4), calls=%async_computation.1 | async-start | bytes 65536 | tf_op jit(solution)/shard_map/all_to_all | solution.py:241

commit v6 on v5

--- a/solution.py
+++ b/solution.py
@@ -15,7 +15,7 @@
 BLOCK = 128
 SPEC = 256
 HALF = BLOCK // 2
-WIDTH = 256
+WIDTH = 512
 VMEM_LIMIT = 40 * 1024 * 1024
 
 
@@ -91,7 +91,7 @@
     )
 
 
-def inner_kernel(gated_ref, mix_ref, fwd_ref, inv_ref, out_ref):
+def inner_kernel(gated_ref, mix_ref, fwd_ref, inv_ref, out_ref, edge_ref):
     fwd, inv = fwd_ref[...], inv_ref[...]
     blocks = gated_ref.shape[0] // BLOCK
     for part in range(gated_ref.shape[1] // WIDTH):
@@ -101,6 +101,8 @@
         for n in range(blocks):
             gated = spectrum(fwd, gated_ref[rows(n), chans])
             grad = spectrum(fwd, mix_ref[rows(n), chans])
+            if n == 0:
+                edge_ref[:BLOCK, chans], edge_ref[BLOCK:, chans] = grad
             window = gated if before is None else beside(gated, before)
             more = correlation_terms(grad, window)
             terms = more if terms is None else tuple(a + b for a, b in zip(terms, more))
@@ -108,14 +110,14 @@
         out_ref[:, chans] = correlation(inv, terms)
 
 
-def outer_kernel(halo_ref, mix_ref, inner_ref, fwd_ref, inv_ref, out_ref):
+def outer_kernel(halo_ref, edge_ref, inner_ref, fwd_ref, inv_ref, out_ref):
     fwd, inv = fwd_ref[...], inv_ref[...]
     for part in range(halo_ref.shape[1] // WIDTH):
         chans = pl.ds(part * WIDTH, WIDTH)
         halo = spectrum(fwd, halo_ref[:, chans])
         zero = jnp.zeros_like(halo[0])
         window = beside((zero, zero), halo)
-        grad = spectrum(fwd, mix_ref[:, chans])
+        grad = edge_ref[:BLOCK, chans], edge_ref[BLOCK:, chans]
         total = inner_ref[:, chans] + correlation(inv, correlation_terms(grad, window))
         for piece in range(WIDTH // 128):
             out_ref[rows(part * (WIDTH // 128) + piece), :] = total[
@@ -197,11 +199,14 @@
     after = jnp.where(first_core, from_inside, from_outside)
 
     close = pl.BlockSpec(memory_space=pltpu.VMEM)
-    inner = pl.pallas_call(
+    inner, edge_spectrum = pl.pallas_call(
         inner_kernel,
         in_specs=[close] * 4,
-        out_specs=close,
-        out_shape=jax.ShapeDtypeStruct((BLOCK, chan_count), F32),
+        out_specs=[close] * 2,
+        out_shape=[
+            jax.ShapeDtypeStruct((BLOCK, chan_count), F32),
+            jax.ShapeDtypeStruct((SPEC, chan_count), F32),
+        ],
         compiler_params=params(),
         cost_estimate=cost(800_000_000, 2_500_000),
         name="inner_pairs",
@@ -215,7 +220,7 @@
         compiler_params=params(),
         cost_estimate=cost(200_000_000, 800_000),
         name="outer_pairs",
-    )(before, mix_edge, inner, fwd, inv)
+    )(before, edge_spectrum, inner, fwd, inv)
 
     near = ("c", "xh", "xl", "y")
     near_count = 1

time: 57.2 us -> 57.1 us (level)
  no operation moved by 1% of the time
where the time goes in v6:
time: 57.1 us; the launch traced here: 56.8 us
  blocking collectives  27.9 us (49%)
  starting transfers between devices  14.3 us (25%)
  Pallas kernels  5.45 us (10%)
  other arithmetic  3.68 us (6%)
  waiting for transfers between devices  3.1 us (5%)
  local copies, waits for them, and re-layouts  1.51 us (3%)
  between operations  0.8 us (1%)
    all_to_all x1, blocking collectives, shards(): lax.all_to_all(chunks, near, 0, 0, tiled=True).astype(F32).sum(axis=0)  15.2 us
    all_to_all x1, blocking collectives, shards(): total = lax.all_to_all(copies, near, 0, 0, tiled=True)  12.7 us
    all_to_all x1, starting transfers between devices, shards(): lax.all_to_all(planes, far, 0, 0, tiled=True).astype(F32).sum(axis=0)  8.19 us
    ppermute x1, starting transfers between devices, shards(): from_outside = lax.ppermute(to_outside, ctx, both_ways[1])  6.04 us
    pallas_call x1, Pallas kernels, shards(): pl.pallas_call(conv_kernel, grid=(1,), in_specs=[stack, stack, whole, who...  3.75 us
    all_to_all x1, waiting for transfers between devices, shards(): lax.all_to_all(planes, far, 0, 0, tiled=True).astype(F32).sum(axis=0)  3.1 us
    convert_element_type x1, other arithmetic, product(): return (left.astype(F32) * right.astype(F32)).astype(BF16)  1.65 us
    select_n x1, other arithmetic, shards(): jnp.where(first_core, product(query_act[0, :BLOCK], grad_out[0, :BLOCK]),...  1.22 us
  transfers between devices with their start and end apart: 3, of which 1 were waited for; matrix products, arithmetic and copies ran while one was open for 3% of the time, Pallas kernels for 9%

profile of v6, /device:TPU:1, one launch (start us, length us, event | category | flops | bytes accessed | tf_op | source)
XLA Modules:
  0.0 56.8 jit_solution(2472108121068239493)
XLA Ops:
  0.6 1.2 %fusion.1 = bf16[128,512]{1,0:T(8,128)(2,1)S(1)} fusion(bf16[1,512,512]{2,1,0:T(8,128)(2,1)} %value_ref.1, bf16[1,512,512]{2,1,0:T(8,128)(2,1)} %key_ref.1, bf16[1,512,512]{2,1,0:T(8,128)(2,1)} %grad_ref.1, bf16[1,512,512]{2,1,0:T(8,128)(2,1)} %param.7, pred[]{:T(512)S(6)} %eq.3), kind=kLoop, calls=%fused_computation.7 | loop fusion | flops 589824 | bytes 655361 | tf_op jit(solution)/shard_map/jit(_where)/select_n | solution.py:192
  1.9 6.0 %collective-permute-start = (bf16[128,512]{1,0:T(8,128)(2,1)S(1)}, bf16[128,512]{1,0:T(8,128)(2,1)S(1)}, u32[]{:S(2)}, u32[]{:S(2)}) collective-permute-start(bf16[128,512]{1,0:T(8,128)(2,1)S(1)} %fusion.1), channel_id=1, source_target_pairs={{8,16},{24,32},{40,48},{56,64},{72,80},{88,96},{104,112},{120,128}... | collective-permute-start | bytes 393224 | tf_op jit(solution)/shard_map/ppermute | solution.py:197
  7.9 1.6 %multiply_convert_fusion = (bf16[1,512,512]{2,1,0:T(8,128)(2,1)S(1)}, bf16[1,512,512]{2,1,0:T(8,128)(2,1)S(1)}) fusion(bf16[1,512,512]{2,1,0:T(8,128)(2,1)S(1)} %copy-done, bf16[1,512,512]{2,1,0:T(8,128)(2,1)} %param.7, bf16[1,512,512]{2,1,0:T(8,128)(2,1)} %value_ref.1, bf16[1,512,512]{2,1,0:T(8,128)(2,1)} %key_ref.1), kind=kLoop, calls=%fused_computation | loop fusion | flops 2097152 | bytes 3145728 | tf_op jit(solution)/shard_map/convert_element_type | solution.py:72
  9.6 0.0 copy-start.3
  9.6 0.0 copy-start.4
  9.6 0.1 collective-permute-start.1
  9.7 0.8 %copy-done.3 = bf16[256,256]{1,0:T(8,128)(2,1)S(1)} copy-done((bf16[256,256]{1,0:T(8,128)(2,1)S(1)}, bf16[256,256]{1,0:T(8,128)(2,1)}, u32[]{:S(2)}) %copy-start.3) | copy-done | bytes 131096
  10.5 0.1 copy-done.4
  10.6 1.2 %inner_pairs.1 = (f32[128,512]{1,0:T(8,128)S(1)}, f32[256,512]{1,0:T(8,128)S(1)}) custom-call(bf16[512,512]{1,0:T(8,128)(2,1)S(1)} %bitcast.13, bf16[512,512]{1,0:T(8,128)(2,1)S(1)} %bitcast.11, bf16[256,256]{1,0:T(8,128)(2,1)S(1)} %copy-done.4, bf16[256,256]{1,0:T(8,128)(2,1)S(1)} %copy-done.3), custom_call_target="tpu_custom_call" | custom-call | flops 800000000 | bytes 2500000 | tf_op jit(solution)/shard_map/inner_pairs/pallas_call | solution.py:202
  11.7 0.0 collective-permute-done
  11.7 0.0 collective-permute-done.1
  11.8 0.0 copy-start.1
  11.8 0.0 copy-start.2
  11.8 0.5 outer_pairs.1
  12.3 15.2 %all_to_all.15 = bf16[32,16,128]{2,1,0:T(8,128)(2,1)S(1)} all-to-all(bf16[32,16,128]{2,1,0:T(8,128)(2,1)S(1)} %bitcast.15), channel_id=1, replica_groups=mesh['z'=8,'xh'=2,'c'=2,'y'=4,'xl'=2] {'c','xh','xl','y'}, dimensions={0} | all-to-all | bytes 262144 | tf_op jit(solution)/shard_map/all_to_all | solution.py:232
  27.6 0.6 %broadcast_in_dim.4 = bf16[8,16,128]{2,1,0:T(8,128)(2,1)} broadcast(bf16[16,128]{1,0:T(8,128)(2,1)S(1)} %convert_reduce_fusion), dimensions={1,2} | broadcast | bytes 36864 | tf_op jit(solution)/shard_map/broadcast_in_dim | solution.py:245
  28.2 8.2 %all-to-all-start.1 = ((bf16[8,16,128]{2,1,0:T(8,128)(2,1)}), bf16[8,16,128]{2,1,0:T(8,128)(2,1)S(1)}, u32[]{:S(2)}, u32[]{:S(2)}) async-start(bf16[8,16,128]{2,1,0:T(8,128)(2,1)} %broadcast_in_dim.4), calls=%async_computation.1 | async-start | bytes 65536 | tf_op jit(solution)/shard_map/all_to_all | solution.py:246
  36.4 0.0 copy-done.1
  36.4 0.0 copy-done.2
  36.4 0.0 copy-done.5
  36.5 3.8 %convolutions.1 = (bf16[1,512,512]{2,1,0:T(8,128)(2,1)}, bf16[1,512,512]{2,1,0:T(8,128)(2,1)}, bf16[1,512,512]{2,1,0:T(8,128)(2,1)}) custom-call(bf16[512,512]{1,0:T(8,128)(2,1)S(1)} %bitcast.14, bf16[512,512]{1,0:T(8,128)(2,1)S(1)} %bitcast.12, bf16[1,512,512]{2,1,0:T(8,128)(2,1)S(1)} %copy-done.2, bf16[1,512,512]{2,1,0:T(8,128)(2,1)S(1)} %copy-done.1, ...), custom_call_target="tpu_custom_call" | custom-call | flops 2000000000 | bytes 4000000 | tf_op jit(solution)/shard_map/convolutions/pallas_call | solution.py:235
  40.2 3.1 %all-to-all-done.1 = bf16[8,16,128]{2,1,0:T(8,128)(2,1)S(1)} async-done(((bf16[8,16,128]{2,1,0:T(8,128)(2,1)}), bf16[8,16,128]{2,1,0:T(8,128)(2,1)S(1)}, u32[]{:S(2)}, u32[]{:S(2)}) %all-to-all-start.1) | async-done | bytes 32800 | tf_op jit(solution)/shard_map/all_to_all | solution.py:246
  43.4 12.7 %all_to_all.16 = bf16[32,16,128]{2,1,0:T(8,128)(2,1)S(1)} all-to-all(bf16[32,16,128]{2,1,0:T(8,128)(2,1)S(1)} %broadcast_in_dim.5), channel_id=1, replica_groups=mesh['z'=8,'xh'=2,'c'=2,'y'=4,'xl'=2] {'c','xh','xl','y'}, dimensions={0} | all-to-all | bytes 262144 | tf_op jit(solution)/shard_map/all_to_all | solution.py:251
  56.1 0.7 %pad_maximum_fusion = f32[128,512]{1,0:T(8,128)} fusion(f32[128,128]{1,0:T(8,128)S(1)} %bitcast.19, f32[128,128]{1,0:T(8,128)S(1)} %bitcast.18, f32[128,128]{1,0:T(8,128)S(1)} %bitcast.17, f32[128,128]{1,0:T(8,128)S(1)} %bitcast.16), kind=kLoop, calls=%fused_computation.2 | loop fusion | flops 196608 | bytes 524288 | tf_op jit(solution)/shard_map/concatenate | solution.py:253
  (10 shorter events, 0.1 us)
Async XLA Ops:
  0.6 7.3 %copy-start = (bf16[1,512,512]{2,1,0:T(8,128)(2,1)S(1)}, bf16[1,512,512]{2,1,0:T(8,128)(2,1)}, u32[]{:S(2)}) copy-start(bf16[1,512,512]{2,1,0:T(8,128)(2,1)} %grad_ref.1) | copy-start | bytes 1572868
  1.9 9.9 %collective-permute-start = (bf16[128,512]{1,0:T(8,128)(2,1)S(1)}, bf16[128,512]{1,0:T(8,128)(2,1)S(1)}, u32[]{:S(2)}, u32[]{:S(2)}) collective-permute-start(bf16[128,512]{1,0:T(8,128)(2,1)S(1)} %fusion.1), channel_id=1, source_target_pairs={{8,16},{24,32},{40,48},{56,64},{72,80},{88,96},{104,112},{120,128}... | collective-permute-start | bytes 393224 | tf_op jit(solution)/shard_map/ppermute | solution.py:197
  9.6 0.9 %copy-start.3 = (bf16[256,256]{1,0:T(8,128)(2,1)S(1)}, bf16[256,256]{1,0:T(8,128)(2,1)}, u32[]{:S(2)}) copy-start(bf16[256,256]{1,0:T(8,128)(2,1)} %constant.18.clone.inv_ref) | copy-start | bytes 393220
  9.6 1.0 %copy-start.4 = (bf16[256,256]{1,0:T(8,128)(2,1)S(1)}, bf16[256,256]{1,0:T(8,128)(2,1)}, u32[]{:S(2)}) copy-start(bf16[256,256]{1,0:T(8,128)(2,1)} %constant.17.clone.fwd_ref) | copy-start | bytes 393220
  9.6 2.1 %collective-permute-start.1 = (bf16[128,512]{1,0:T(8,128)(2,1)S(1)}, bf16[128,512]{1,0:T(8,128)(2,1)S(1)}, u32[]{:S(2)}, u32[]{:S(2)}) collective-permute-start(bf16[128,512]{1,0:T(8,128)(2,1)S(1)} %fusion.2), channel_id=1, source_target_pairs={{0,8},{16,24},{32,40},{48,56},{64,72},{80,88},{96,104},{112,120},{... | collective-permute-start | bytes 393224 | tf_op jit(solution)/shard_map/ppermute | solution.py:191
  11.8 24.7 %copy-start.1 = (bf16[1,512,512]{2,1,0:T(8,128)(2,1)S(1)}, bf16[1,512,512]{2,1,0:T(8,128)(2,1)}, u32[]{:S(2)}) copy-start(bf16[1,512,512]{2,1,0:T(8,128)(2,1)} %value_ref.1) | copy-start | bytes 1572868
  11.8 24.6 %copy-start.2 = (bf16[1,512,512]{2,1,0:T(8,128)(2,1)S(1)}, bf16[1,512,512]{2,1,0:T(8,128)(2,1)}, u32[]{:S(2)}) copy-start(bf16[1,512,512]{2,1,0:T(8,128)(2,1)} %key_ref.1) | copy-start | bytes 1572868
  27.6 8.9 %copy-start.5 = (bf16[128,512]{1,0:T(8,128)(2,1)S(1)}, bf16[128,512]{1,0:T(8,128)(2,1)}, u32[]{:S(2)}) copy-start(bf16[128,512]{1,0:T(8,128)(2,1)} %taps_ref.1) | copy-start | bytes 393220
  28.2 15.1 %all-to-all-start.1 = ((bf16[8,16,128]{2,1,0:T(8,128)(2,1)}), bf16[8,16,128]{2,1,0:T(8,128)(2,1)S(1)}, u32[]{:S(2)}, u32[]{:S(2)}) async-start(bf16[8,16,128]{2,1,0:T(8,128)(2,1)} %broadcast_in_dim.4), calls=%async_computation.1 | async-start | bytes 65536 | tf_op jit(solution)/shard_map/all_to_all | solution.py:246

commit v7 on v6

--- a/solution.py
+++ b/solution.py
@@ -156,6 +156,12 @@
     backward(blocks - 1, earlier, spectrum(fwd, after_ref[...]))
 
 
+def spread_kernel(terms_ref, out_ref):
+    total = jnp.sum(terms_ref[...].astype(F32), axis=0).astype(BF16)
+    for place in range(out_ref.shape[0]):
+        out_ref[place] = total
+
+
 def params():
     return pltpu.CompilerParams(vmem_limit_bytes=VMEM_LIMIT)
 
@@ -222,14 +228,14 @@
         name="outer_pairs",
     )(before, edge_spectrum, inner, fwd, inv)
 
-    near = ("c", "xh", "xl", "y")
+    near = ("c", "y", "xh", "xl")
     near_count = 1
     for name in near:
         near_count *= lax.axis_size(name)
     far = "z"
     far_count = lax.axis_size(far)
     chunks = partial.reshape(near_count, -1, 128)
-    mine = lax.all_to_all(chunks, near, 0, 0, tiled=True).astype(F32).sum(axis=0)
+    mine = lax.all_to_all(chunks, near, 0, 0, tiled=True)
     mine, before, after = lax.optimization_barrier((mine, before, after))
     out_shape = jax.ShapeDtypeStruct(query_act.shape, BF16)
     grad_query, grad_key, grad_value = pl.pallas_call(
@@ -242,7 +248,15 @@
         cost_estimate=cost(2_000_000_000, 4_000_000),
         name="convolutions",
     )(gated, mix, key_act, value_act, grad_out, before, after, filter_taps, fwd, inv)
-    planes = jnp.broadcast_to(mine.astype(BF16)[None], (far_count,) + mine.shape)
+    planes = pl.pallas_call(
+        spread_kernel,
+        in_specs=[close],
+        out_specs=close,
+        out_shape=jax.ShapeDtypeStruct((far_count,) + mine.shape[1:], BF16),
+        compiler_params=params(),
+        cost_estimate=cost(100_000, 200_000),
+        name="spread",
+    )(mine)
     mine = lax.all_to_all(planes, far, 0, 0, tiled=True).astype(F32).sum(axis=0) / math.sqrt(count_all)
     mine, grad_query, grad_key, grad_value = lax.optimization_barrier(
         (mine, grad_query, grad_key, grad_value)

time: 57.1 us -> 57.1 us (level)
  Pallas kernels: 5.45 us -> 6.1 us
  local copies, waits for them, and re-layouts: 1.51 us -> 0.89 us
    pallas_call x0 -> x1, Pallas kernels: none -> 0.65 us  [shards(): pl.pallas_call(spread_kernel, in_specs=[close], out_specs=close, out_shap...]
    broadcast_in_dim x1 -> x0, local copies, waits for them, and re-layouts: 0.62 us -> none  [shards(): jnp.broadcast_to(mine.astype(BF16)[None], (far_count,) + mine.shape)]
where the time goes in v7:
time: 57.1 us; the launch traced here: 56.7 us
  blocking collectives  27.9 us (49%)
  starting transfers between devices  14.3 us (25%)
  Pallas kernels  6.1 us (11%)
  other arithmetic  3.64 us (6%)
  waiting for transfers between devices  3.1 us (5%)
  local copies, waits for them, and re-layouts  0.89 us (2%)
  between operations  0.8 us (1%)
    all_to_all x1, blocking collectives, shards(): mine = lax.all_to_all(chunks, near, 0, 0, tiled=True)  15.2 us
    all_to_all x1, blocking collectives, shards(): total = lax.all_to_all(copies, near, 0, 0, tiled=True)  12.6 us
    all_to_all x1, starting transfers between devices, shards(): lax.all_to_all(planes, far, 0, 0, tiled=True).astype(F32).sum(axis=0)  8.19 us
    ppermute x1, starting transfers between devices, shards(): from_outside = lax.ppermute(to_outside, ctx, both_ways[1])  6.04 us
    pallas_call x1, Pallas kernels, shards(): pl.pallas_call(conv_kernel, grid=(1,), in_specs=[stack, stack, whole, who...  3.76 us
    all_to_all x1, waiting for transfers between devices, shards(): lax.all_to_all(planes, far, 0, 0, tiled=True).astype(F32).sum(axis=0)  3.1 us
    convert_element_type x1, other arithmetic, product(): return (left.astype(F32) * right.astype(F32)).astype(BF16)  1.65 us
    select_n x1, other arithmetic, shards(): jnp.where(first_core, product(query_act[0, :BLOCK], grad_out[0, :BLOCK]),...  1.22 us
  transfers between devices with their start and end apart: 3, of which 1 were waited for; matrix products, arithmetic and copies ran while one was open for 3% of the time, Pallas kernels for 9%

profile of v7, /device:TPU:1, one launch (start us, length us, event | category | flops | bytes accessed | tf_op | source)
XLA Modules:
  0.0 56.7 jit_solution(14360392399776767987)
XLA Ops:
  0.6 0.0 copy-start
  0.6 1.2 %fusion.1 = bf16[128,512]{1,0:T(8,128)(2,1)S(1)} fusion(bf16[1,512,512]{2,1,0:T(8,128)(2,1)} %value_ref.1, bf16[1,512,512]{2,1,0:T(8,128)(2,1)} %key_ref.1, bf16[1,512,512]{2,1,0:T(8,128)(2,1)} %grad_ref.1, bf16[1,512,512]{2,1,0:T(8,128)(2,1)} %param.7, pred[]{:T(512)S(6)} %eq.3), kind=kLoop, calls=%fused_computation.6 | loop fusion | flops 589824 | bytes 655361 | tf_op jit(solution)/shard_map/jit(_where)/select_n | solution.py:198
  1.9 6.0 %collective-permute-start = (bf16[128,512]{1,0:T(8,128)(2,1)S(1)}, bf16[128,512]{1,0:T(8,128)(2,1)S(1)}, u32[]{:S(2)}, u32[]{:S(2)}) collective-permute-start(bf16[128,512]{1,0:T(8,128)(2,1)S(1)} %fusion.1), channel_id=1, source_target_pairs={{8,16},{24,32},{40,48},{56,64},{72,80},{88,96},{104,112},{120,128}... | collective-permute-start | bytes 393224 | tf_op jit(solution)/shard_map/ppermute | solution.py:203
  7.9 0.0 copy-done
  7.9 1.6 %multiply_convert_fusion = (bf16[1,512,512]{2,1,0:T(8,128)(2,1)S(1)}, bf16[1,512,512]{2,1,0:T(8,128)(2,1)S(1)}) fusion(bf16[1,512,512]{2,1,0:T(8,128)(2,1)S(1)} %copy-done, bf16[1,512,512]{2,1,0:T(8,128)(2,1)} %param.7, bf16[1,512,512]{2,1,0:T(8,128)(2,1)} %value_ref.1, bf16[1,512,512]{2,1,0:T(8,128)(2,1)} %key_ref.1), kind=kLoop, calls=%fused_computation | loop fusion | flops 2097152 | bytes 3145728 | tf_op jit(solution)/shard_map/convert_element_type | solution.py:72
  9.6 0.0 copy-start.3
  9.6 0.0 copy-start.4
  9.6 0.1 collective-permute-start.1
  9.7 0.8 %copy-done.3 = bf16[256,256]{1,0:T(8,128)(2,1)S(1)} copy-done((bf16[256,256]{1,0:T(8,128)(2,1)S(1)}, bf16[256,256]{1,0:T(8,128)(2,1)}, u32[]{:S(2)}) %copy-start.3) | copy-done | bytes 131096
  10.5 0.1 copy-done.4
  10.6 1.2 %inner_pairs.1 = (f32[128,512]{1,0:T(8,128)S(1)}, f32[256,512]{1,0:T(8,128)S(1)}) custom-call(bf16[512,512]{1,0:T(8,128)(2,1)S(1)} %bitcast.13, bf16[512,512]{1,0:T(8,128)(2,1)S(1)} %bitcast.11, bf16[256,256]{1,0:T(8,128)(2,1)S(1)} %copy-done.4, bf16[256,256]{1,0:T(8,128)(2,1)S(1)} %copy-done.3), custom_call_target="tpu_custom_call" | custom-call | flops 800000000 | bytes 2500000 | tf_op jit(solution)/shard_map/inner_pairs/pallas_call | solution.py:208
  11.7 0.0 collective-permute-done
  11.7 0.0 collective-permute-done.1
  11.8 0.0 copy-start.1
  11.8 0.0 copy-start.2
  11.8 0.5 outer_pairs.1
  12.3 15.2 %all_to_all.15.terms_ref = bf16[32,16,128]{2,1,0:T(8,128)(2,1)S(1)} all-to-all(bf16[32,16,128]{2,1,0:T(8,128)(2,1)S(1)} %bitcast.15), channel_id=1, replica_groups=mesh['z'=8,'xh'=2,'c'=2,'y'=4,'xl'=2] {'c','y','xh','xl'}, dimensions={0} | all-to-all | bytes 262144 | tf_op jit(solution)/shard_map/all_to_all | solution.py:238
  27.6 0.7 %spread.1 = bf16[8,16,128]{2,1,0:T(8,128)(2,1)} custom-call(bf16[32,16,128]{2,1,0:T(8,128)(2,1)S(1)} %all_to_all.15.terms_ref), custom_call_target="tpu_custom_call" | custom-call | flops 100000 | bytes 200000 | tf_op jit(solution)/shard_map/spread/pallas_call | solution.py:251
  28.2 8.2 %all-to-all-start.1 = ((bf16[8,16,128]{2,1,0:T(8,128)(2,1)}), bf16[8,16,128]{2,1,0:T(8,128)(2,1)S(1)}, u32[]{:S(2)}, u32[]{:S(2)}) async-start(bf16[8,16,128]{2,1,0:T(8,128)(2,1)} %spread.1), calls=%async_computation.1 | async-start | bytes 65536 | tf_op jit(solution)/shard_map/all_to_all | solution.py:260
  36.4 0.0 copy-done.1
  36.4 3.8 %convolutions.1 = (bf16[1,512,512]{2,1,0:T(8,128)(2,1)}, bf16[1,512,512]{2,1,0:T(8,128)(2,1)}, bf16[1,512,512]{2,1,0:T(8,128)(2,1)}) custom-call(bf16[512,512]{1,0:T(8,128)(2,1)S(1)} %bitcast.14, bf16[512,512]{1,0:T(8,128)(2,1)S(1)} %bitcast.12, bf16[1,512,512]{2,1,0:T(8,128)(2,1)S(1)} %copy-done.2, bf16[1,512,512]{2,1,0:T(8,128)(2,1)S(1)} %copy-done.1, ...), custom_call_target="tpu_custom_call" | custom-call | flops 2000000000 | bytes 4000000 | tf_op jit(solution)/shard_map/convolutions/pallas_call | solution.py:241
  40.2 3.1 %all-to-all-done.1 = bf16[8,16,128]{2,1,0:T(8,128)(2,1)S(1)} async-done(((bf16[8,16,128]{2,1,0:T(8,128)(2,1)}), bf16[8,16,128]{2,1,0:T(8,128)(2,1)S(1)}, u32[]{:S(2)}, u32[]{:S(2)}) %all-to-all-start.1) | async-done | bytes 32800 | tf_op jit(solution)/shard_map/all_to_all | solution.py:260
  43.3 12.6 %all_to_all.16 = bf16[32,16,128]{2,1,0:T(8,128)(2,1)S(1)} all-to-all(bf16[32,16,128]{2,1,0:T(8,128)(2,1)S(1)} %broadcast_in_dim.2), channel_id=1, replica_groups=mesh['z'=8,'xh'=2,'c'=2,'y'=4,'xl'=2] {'c','y','xh','xl'}, dimensions={0} | all-to-all | bytes 262144 | tf_op jit(solution)/shard_map/all_to_all | solution.py:265
  56.0 0.7 %pad_maximum_fusion = f32[128,512]{1,0:T(8,128)} fusion(f32[128,128]{1,0:T(8,128)S(1)} %bitcast.19, f32[128,128]{1,0:T(8,128)S(1)} %bitcast.18, f32[128,128]{1,0:T(8,128)S(1)} %bitcast.17, f32[128,128]{1,0:T(8,128)S(1)} %bitcast.16), kind=kLoop, calls=%fused_computation.2 | loop fusion | flops 196608 | bytes 524288 | tf_op jit(solution)/shard_map/concatenate | solution.py:267
  (9 shorter events, 0.1 us)
Async XLA Ops:
  0.6 7.3 %copy-start = (bf16[1,512,512]{2,1,0:T(8,128)(2,1)S(1)}, bf16[1,512,512]{2,1,0:T(8,128)(2,1)}, u32[]{:S(2)}) copy-start(bf16[1,512,512]{2,1,0:T(8,128)(2,1)} %grad_ref.1) | copy-start | bytes 1572868
  1.9 9.9 %collective-permute-start = (bf16[128,512]{1,0:T(8,128)(2,1)S(1)}, bf16[128,512]{1,0:T(8,128)(2,1)S(1)}, u32[]{:S(2)}, u32[]{:S(2)}) collective-permute-start(bf16[128,512]{1,0:T(8,128)(2,1)S(1)} %fusion.1), channel_id=1, source_target_pairs={{8,16},{24,32},{40,48},{56,64},{72,80},{88,96},{104,112},{120,128}... | collective-permute-start | bytes 393224 | tf_op jit(solution)/shard_map/ppermute | solution.py:203
  9.6 0.9 %copy-start.3 = (bf16[256,256]{1,0:T(8,128)(2,1)S(1)}, bf16[256,256]{1,0:T(8,128)(2,1)}, u32[]{:S(2)}) copy-start(bf16[256,256]{1,0:T(8,128)(2,1)} %constant.18.clone.inv_ref) | copy-start | bytes 393220
  9.6 1.0 %copy-start.4 = (bf16[256,256]{1,0:T(8,128)(2,1)S(1)}, bf16[256,256]{1,0:T(8,128)(2,1)}, u32[]{:S(2)}) copy-start(bf16[256,256]{1,0:T(8,128)(2,1)} %constant.17.clone.fwd_ref) | copy-start | bytes 393220
  9.6 2.1 %collective-permute-start.1 = (bf16[128,512]{1,0:T(8,128)(2,1)S(1)}, bf16[128,512]{1,0:T(8,128)(2,1)S(1)}, u32[]{:S(2)}, u32[]{:S(2)}) collective-permute-start(bf16[128,512]{1,0:T(8,128)(2,1)S(1)} %fusion.2), channel_id=1, source_target_pairs={{0,8},{16,24},{32,40},{48,56},{64,72},{80,88},{96,104},{112,120},{... | collective-permute-start | bytes 393224 | tf_op jit(solution)/shard_map/ppermute | solution.py:197
  11.8 24.6 %copy-start.1 = (bf16[1,512,512]{2,1,0:T(8,128)(2,1)S(1)}, bf16[1,512,512]{2,1,0:T(8,128)(2,1)}, u32[]{:S(2)}) copy-start(bf16[1,512,512]{2,1,0:T(8,128)(2,1)} %value_ref.1) | copy-start | bytes 1572868
  11.8 24.6 %copy-start.2 = (bf16[1,512,512]{2,1,0:T(8,128)(2,1)S(1)}, bf16[1,512,512]{2,1,0:T(8,128)(2,1)}, u32[]{:S(2)}) copy-start(bf16[1,512,512]{2,1,0:T(8,128)(2,1)} %key_ref.1) | copy-start | bytes 1572868
  27.6 8.9 %copy-start.5 = (bf16[128,512]{1,0:T(8,128)(2,1)S(1)}, bf16[128,512]{1,0:T(8,128)(2,1)}, u32[]{:S(2)}) copy-start(bf16[128,512]{1,0:T(8,128)(2,1)} %taps_ref.1) | copy-start | bytes 393220
  28.2 15.1 %all-to-all-start.1 = ((bf16[8,16,128]{2,1,0:T(8,128)(2,1)}), bf16[8,16,128]{2,1,0:T(8,128)(2,1)S(1)}, u32[]{:S(2)}, u32[]{:S(2)}) async-start(bf16[8,16,128]{2,1,0:T(8,128)(2,1)} %spread.1), calls=%async_computation.1 | async-start | bytes 65536 | tf_op jit(solution)/shard_map/all_to_all | solution.py:260

commit v8 on v6

--- a/solution.py
+++ b/solution.py
@@ -115,8 +115,7 @@
     for part in range(halo_ref.shape[1] // WIDTH):
         chans = pl.ds(part * WIDTH, WIDTH)
         halo = spectrum(fwd, halo_ref[:, chans])
-        zero = jnp.zeros_like(halo[0])
-        window = beside((zero, zero), halo)
+        window = [jnp.concatenate([a[:HALF], -a[HALF:]], axis=0) for a in halo]
         grad = edge_ref[:BLOCK, chans], edge_ref[BLOCK:, chans]
         total = inner_ref[:, chans] + correlation(inv, correlation_terms(grad, window))
         for piece in range(WIDTH // 128):

time: 57.1 us -> 57.1 us (level)
  no operation moved by 1% of the time
where the time goes in v8:
time: 57.1 us; the launch traced here: 56.8 us
  blocking collectives  27.9 us (49%)
  starting transfers between devices  14.3 us (25%)
  Pallas kernels  5.45 us (10%)
  other arithmetic  3.68 us (6%)
  waiting for transfers between devices  3.1 us (5%)
  local copies, waits for them, and re-layouts  1.51 us (3%)
  between operations  0.8 us (1%)
    all_to_all x1, blocking collectives, shards(): lax.all_to_all(chunks, near, 0, 0, tiled=True).astype(F32).sum(axis=0)  15.2 us
    all_to_all x1, blocking collectives, shards(): total = lax.all_to_all(copies, near, 0, 0, tiled=True)  12.7 us
    all_to_all x1, starting transfers between devices, shards(): lax.all_to_all(planes, far, 0, 0, tiled=True).astype(F32).sum(axis=0)  8.19 us
    ppermute x1, starting transfers between devices, shards(): from_outside = lax.ppermute(to_outside, ctx, both_ways[1])  6.04 us
    pallas_call x1, Pallas kernels, shards(): pl.pallas_call(conv_kernel, grid=(1,), in_specs=[stack, stack, whole, who...  3.75 us
    all_to_all x1, waiting for transfers between devices, shards(): lax.all_to_all(planes, far, 0, 0, tiled=True).astype(F32).sum(axis=0)  3.1 us
    convert_element_type x1, other arithmetic, product(): return (left.astype(F32) * right.astype(F32)).astype(BF16)  1.65 us
    select_n x1, other arithmetic, shards(): jnp.where(first_core, product(query_act[0, :BLOCK], grad_out[0, :BLOCK]),...  1.22 us
  transfers between devices with their start and end apart: 3, of which 1 were waited for; matrix products, arithmetic and copies ran while one was open for 3% of the time, Pallas kernels for 9%

profile of v8, /device:TPU:1, one launch (start us, length us, event | category | flops | bytes accessed | tf_op | source)
XLA Modules:
  0.0 56.8 jit_solution(2472108121068239493)
XLA Ops:
  0.6 1.2 %fusion.1 = bf16[128,512]{1,0:T(8,128)(2,1)S(1)} fusion(bf16[1,512,512]{2,1,0:T(8,128)(2,1)} %value_ref.1, bf16[1,512,512]{2,1,0:T(8,128)(2,1)} %key_ref.1, bf16[1,512,512]{2,1,0:T(8,128)(2,1)} %grad_ref.1, bf16[1,512,512]{2,1,0:T(8,128)(2,1)} %param.7, pred[]{:T(512)S(6)} %eq.3), kind=kLoop, calls=%fused_computation.7 | loop fusion | flops 589824 | bytes 655361 | tf_op jit(solution)/shard_map/jit(_where)/select_n | solution.py:191
  1.9 6.0 %collective-permute-start = (bf16[128,512]{1,0:T(8,128)(2,1)S(1)}, bf16[128,512]{1,0:T(8,128)(2,1)S(1)}, u32[]{:S(2)}, u32[]{:S(2)}) collective-permute-start(bf16[128,512]{1,0:T(8,128)(2,1)S(1)} %fusion.1), channel_id=1, source_target_pairs={{8,16},{24,32},{40,48},{56,64},{72,80},{88,96},{104,112},{120,128}... | collective-permute-start | bytes 393224 | tf_op jit(solution)/shard_map/ppermute | solution.py:196
  7.9 1.6 %multiply_convert_fusion = (bf16[1,512,512]{2,1,0:T(8,128)(2,1)S(1)}, bf16[1,512,512]{2,1,0:T(8,128)(2,1)S(1)}) fusion(bf16[1,512,512]{2,1,0:T(8,128)(2,1)S(1)} %copy-done, bf16[1,512,512]{2,1,0:T(8,128)(2,1)} %param.7, bf16[1,512,512]{2,1,0:T(8,128)(2,1)} %value_ref.1, bf16[1,512,512]{2,1,0:T(8,128)(2,1)} %key_ref.1), kind=kLoop, calls=%fused_computation | loop fusion | flops 2097152 | bytes 3145728 | tf_op jit(solution)/shard_map/convert_element_type | solution.py:72
  9.6 0.0 copy-start.3
  9.6 0.0 copy-start.4
  9.6 0.1 collective-permute-start.1
  9.7 0.8 %copy-done.3 = bf16[256,256]{1,0:T(8,128)(2,1)S(1)} copy-done((bf16[256,256]{1,0:T(8,128)(2,1)S(1)}, bf16[256,256]{1,0:T(8,128)(2,1)}, u32[]{:S(2)}) %copy-start.3) | copy-done | bytes 131096
  10.5 0.1 copy-done.4
  10.6 1.2 %inner_pairs.1 = (f32[128,512]{1,0:T(8,128)S(1)}, f32[256,512]{1,0:T(8,128)S(1)}) custom-call(bf16[512,512]{1,0:T(8,128)(2,1)S(1)} %bitcast.13, bf16[512,512]{1,0:T(8,128)(2,1)S(1)} %bitcast.11, bf16[256,256]{1,0:T(8,128)(2,1)S(1)} %copy-done.4, bf16[256,256]{1,0:T(8,128)(2,1)S(1)} %copy-done.3), custom_call_target="tpu_custom_call" | custom-call | flops 800000000 | bytes 2500000 | tf_op jit(solution)/shard_map/inner_pairs/pallas_call | solution.py:201
  11.7 0.0 collective-permute-done
  11.7 0.0 collective-permute-done.1
  11.8 0.0 copy-start.1
  11.8 0.0 copy-start.2
  11.8 0.5 outer_pairs.1
  12.3 15.2 %all_to_all.15 = bf16[32,16,128]{2,1,0:T(8,128)(2,1)S(1)} all-to-all(bf16[32,16,128]{2,1,0:T(8,128)(2,1)S(1)} %bitcast.15), channel_id=1, replica_groups=mesh['z'=8,'xh'=2,'c'=2,'y'=4,'xl'=2] {'c','xh','xl','y'}, dimensions={0} | all-to-all | bytes 262144 | tf_op jit(solution)/shard_map/all_to_all | solution.py:231
  27.6 0.6 %broadcast_in_dim.4 = bf16[8,16,128]{2,1,0:T(8,128)(2,1)} broadcast(bf16[16,128]{1,0:T(8,128)(2,1)S(1)} %convert_reduce_fusion), dimensions={1,2} | broadcast | bytes 36864 | tf_op jit(solution)/shard_map/broadcast_in_dim | solution.py:244
  28.2 8.2 %all-to-all-start.1 = ((bf16[8,16,128]{2,1,0:T(8,128)(2,1)}), bf16[8,16,128]{2,1,0:T(8,128)(2,1)S(1)}, u32[]{:S(2)}, u32[]{:S(2)}) async-start(bf16[8,16,128]{2,1,0:T(8,128)(2,1)} %broadcast_in_dim.4), calls=%async_computation.1 | async-start | bytes 65536 | tf_op jit(solution)/shard_map/all_to_all | solution.py:245
  36.4 0.0 copy-done.1
  36.4 0.0 copy-done.2
  36.4 0.0 copy-done.5
  36.5 3.8 %convolutions.1 = (bf16[1,512,512]{2,1,0:T(8,128)(2,1)}, bf16[1,512,512]{2,1,0:T(8,128)(2,1)}, bf16[1,512,512]{2,1,0:T(8,128)(2,1)}) custom-call(bf16[512,512]{1,0:T(8,128)(2,1)S(1)} %bitcast.14, bf16[512,512]{1,0:T(8,128)(2,1)S(1)} %bitcast.12, bf16[1,512,512]{2,1,0:T(8,128)(2,1)S(1)} %copy-done.2, bf16[1,512,512]{2,1,0:T(8,128)(2,1)S(1)} %copy-done.1, ...), custom_call_target="tpu_custom_call" | custom-call | flops 2000000000 | bytes 4000000 | tf_op jit(solution)/shard_map/convolutions/pallas_call | solution.py:234
  40.2 3.1 %all-to-all-done.1 = bf16[8,16,128]{2,1,0:T(8,128)(2,1)S(1)} async-done(((bf16[8,16,128]{2,1,0:T(8,128)(2,1)}), bf16[8,16,128]{2,1,0:T(8,128)(2,1)S(1)}, u32[]{:S(2)}, u32[]{:S(2)}) %all-to-all-start.1) | async-done | bytes 32800 | tf_op jit(solution)/shard_map/all_to_all | solution.py:245
  43.4 12.7 %all_to_all.16 = bf16[32,16,128]{2,1,0:T(8,128)(2,1)S(1)} all-to-all(bf16[32,16,128]{2,1,0:T(8,128)(2,1)S(1)} %broadcast_in_dim.5), channel_id=1, replica_groups=mesh['z'=8,'xh'=2,'c'=2,'y'=4,'xl'=2] {'c','xh','xl','y'}, dimensions={0} | all-to-all | bytes 262144 | tf_op jit(solution)/shard_map/all_to_all | solution.py:250
  56.1 0.7 %pad_maximum_fusion = f32[128,512]{1,0:T(8,128)} fusion(f32[128,128]{1,0:T(8,128)S(1)} %bitcast.19, f32[128,128]{1,0:T(8,128)S(1)} %bitcast.18, f32[128,128]{1,0:T(8,128)S(1)} %bitcast.17, f32[128,128]{1,0:T(8,128)S(1)} %bitcast.16), kind=kLoop, calls=%fused_computation.2 | loop fusion | flops 196608 | bytes 524288 | tf_op jit(solution)/shard_map/concatenate | solution.py:252
  (10 shorter events, 0.1 us)
Async XLA Ops:
  0.6 7.3 %copy-start = (bf16[1,512,512]{2,1,0:T(8,128)(2,1)S(1)}, bf16[1,512,512]{2,1,0:T(8,128)(2,1)}, u32[]{:S(2)}) copy-start(bf16[1,512,512]{2,1,0:T(8,128)(2,1)} %grad_ref.1) | copy-start | bytes 1572868
  1.9 9.9 %collective-permute-start = (bf16[128,512]{1,0:T(8,128)(2,1)S(1)}, bf16[128,512]{1,0:T(8,128)(2,1)S(1)}, u32[]{:S(2)}, u32[]{:S(2)}) collective-permute-start(bf16[128,512]{1,0:T(8,128)(2,1)S(1)} %fusion.1), channel_id=1, source_target_pairs={{8,16},{24,32},{40,48},{56,64},{72,80},{88,96},{104,112},{120,128}... | collective-permute-start | bytes 393224 | tf_op jit(solution)/shard_map/ppermute | solution.py:196
  9.6 0.9 %copy-start.3 = (bf16[256,256]{1,0:T(8,128)(2,1)S(1)}, bf16[256,256]{1,0:T(8,128)(2,1)}, u32[]{:S(2)}) copy-start(bf16[256,256]{1,0:T(8,128)(2,1)} %constant.18.clone.inv_ref) | copy-start | bytes 393220
  9.6 1.0 %copy-start.4 = (bf16[256,256]{1,0:T(8,128)(2,1)S(1)}, bf16[256,256]{1,0:T(8,128)(2,1)}, u32[]{:S(2)}) copy-start(bf16[256,256]{1,0:T(8,128)(2,1)} %constant.17.clone.fwd_ref) | copy-start | bytes 393220
  9.6 2.1 %collective-permute-start.1 = (bf16[128,512]{1,0:T(8,128)(2,1)S(1)}, bf16[128,512]{1,0:T(8,128)(2,1)S(1)}, u32[]{:S(2)}, u32[]{:S(2)}) collective-permute-start(bf16[128,512]{1,0:T(8,128)(2,1)S(1)} %fusion.2), channel_id=1, source_target_pairs={{0,8},{16,24},{32,40},{48,56},{64,72},{80,88},{96,104},{112,120},{... | collective-permute-start | bytes 393224 | tf_op jit(solution)/shard_map/ppermute | solution.py:190
  11.8 24.7 %copy-start.1 = (bf16[1,512,512]{2,1,0:T(8,128)(2,1)S(1)}, bf16[1,512,512]{2,1,0:T(8,128)(2,1)}, u32[]{:S(2)}) copy-start(bf16[1,512,512]{2,1,0:T(8,128)(2,1)} %value_ref.1) | copy-start | bytes 1572868
  11.8 24.6 %copy-start.2 = (bf16[1,512,512]{2,1,0:T(8,128)(2,1)S(1)}, bf16[1,512,512]{2,1,0:T(8,128)(2,1)}, u32[]{:S(2)}) copy-start(bf16[1,512,512]{2,1,0:T(8,128)(2,1)} %key_ref.1) | copy-start | bytes 1572868
  27.6 8.9 %copy-start.5 = (bf16[128,512]{1,0:T(8,128)(2,1)S(1)}, bf16[128,512]{1,0:T(8,128)(2,1)}, u32[]{:S(2)}) copy-start(bf16[128,512]{1,0:T(8,128)(2,1)} %taps_ref.1) | copy-start | bytes 393220
  28.2 15.1 %all-to-all-start.1 = ((bf16[8,16,128]{2,1,0:T(8,128)(2,1)}), bf16[8,16,128]{2,1,0:T(8,128)(2,1)S(1)}, u32[]{:S(2)}, u32[]{:S(2)}) async-start(bf16[8,16,128]{2,1,0:T(8,128)(2,1)} %broadcast_in_dim.4), calls=%async_computation.1 | async-start | bytes 65536 | tf_op jit(solution)/shard_map/all_to_all | solution.py:245
